TPU v7x, 32 devices: a whole 2x2x4 slice. The times are simulated.
32 devices in a mesh: gx: 4 (over z), gy: 8 (over y, x, core).
Axes of the slice: x: 2, y: 2, z: 4, core: 2. Of those that a mesh axis runs over, the one named last changes fastest.
Arguments:
- depth: float32 [1024, 128, 128], P(('gx', 'gy')), may hold values from 0.1 to 2
- discharge: float32 [1024, 2, 128, 128], P(('gx', 'gy')), may hold values from -3 to 3
- bed: float32 [1024, 128, 128], P(('gx', 'gy')), may hold values from -1.5 to 2.5
- friction: float32 [1024, 128, 128], P(('gx', 'gy')), may hold values from 0.004 to 0.1
- tile_ids: int32 [1024], P(('gx', 'gy')), may hold values from -1 to 1023, as said below
- neighbors: int32 [1024, 4], P(('gx', 'gy')), may hold values from -1 to 1023, as said below
- moves: int32 [32, 2, 8, 2], P(('gx', 'gy')), may hold values from -1 to 1023, as said below
Outputs:
- new_depth: float32 [1024, 128, 128], P(('gx', 'gy'))
- new_discharge: float32 [1024, 2, 128, 128], P(('gx', 'gy'))
Inputs may be any that keep to these rules, and one draw needn't show every extreme that they name: `tile_ids`: each owner's wet tiles after the moves fill its first slots: those that stayed, in curve order, then those arrived from lower gy, then those arrived from higher gy; an empty slot is -1. `neighbors`: links are symmetric and join only slots with tile_ids >= 0. The tile beside on side 0 or 1 is held by the same owner or by the owner at gx - 1 or gx + 1 respectively; on side 2 or 3 by the same owner or the owner at gy - 1 or gy + 1. At most 4 tiles of an owner have their side 0 (or side 1) neighbour on another owner, and at most 8 their side 2 (or side 3) neighbour; both bounds are reached on some owner. Entries are global slots, -1 if unused, used entries first. Leaving slots lie on the owner and hold no tile that stays; landing slots lie on the owner and are either left by a tile or hold no tile before the moves. The m-th tile leaving owner (a, b) toward higher gy is the m-th arriving at (a, b + 1) from lower gy, and likewise downward; owners at the ends of gy list nothing toward the outside. All 8 entries of a direction are used on some owners.
All inputs are finite; a program needn't handle non-finite values.
Results may differ from a plain program's by a relative error of at most 0.00002.
Values sent between devices are 32-bit elements; how exact they have to be, the bound alone decides.
A program may use at most 128 MiB of HBM per device.

v0:
```python
import jax
import jax.numpy as jnp
from jax import lax
from jax.sharding import PartitionSpec as P

BLOCK_ROWS = 8
BLOCK_COLS = 4
STEPS = 4


gravity = 9.81
step_time = 0.25
spacing = 2.0
min_depth = 0.15


def shifted(block, axis, distance):
    devices = range(lax.axis_size(axis))
    route = [(i - distance, i) for i in devices if i - distance in devices]
    return lax.ppermute(block, axis, route)


def with_halo(block, sides, width):
    for axis, dim in sides:
        count = lax.axis_size(axis)
        forward = [(i, i + 1) for i in range(count - 1)]
        backward = [(target, source) for source, target in forward]
        low = lax.ppermute(
            lax.slice_in_dim(block, block.shape[dim] - width, None, axis=dim), axis, forward
        )
        high = lax.ppermute(lax.slice_in_dim(block, 0, width, axis=dim), axis, backward)
        block = jnp.concatenate([low, block, high], axis=dim)
    return block


def face_flux(flow, h_lo, h_hi, z_lo, z_hi, n_lo, n_hi):
    depth_face = jnp.maximum(0.5 * (h_lo + h_hi), min_depth)
    drive = flow - gravity * step_time / spacing * depth_face * (h_hi + z_hi - (h_lo + z_lo))
    drag = 1.0 + gravity * step_time * 0.5 * (n_lo + n_hi) * jnp.abs(flow) * jnp.exp(
        -(7.0 / 3.0) * jnp.log(depth_face)
    )
    return drive / drag


def pass_along_gx(rows, shift_by):
    return shifted(rows, "gx", shift_by)


def pass_along_gy(rows, shift_by):
    return shifted(rows, "gy", shift_by)


def pick_rows(rows, wanted, count):
    order = jnp.cumsum(wanted.astype(jnp.int32)) - 1
    hit = wanted[None, :] & (order[None, :] == jnp.arange(count)[:, None])
    chosen = jnp.sum(jnp.where(hit, jnp.arange(wanted.shape[0])[None, :], 0), 1)
    return jnp.take(rows, chosen, axis=0)


def place_rows(arrived, rows, link, owner_id, base):
    slots = rows.shape[0]
    exists = link >= 0
    local = exists & (link // slots == owner_id)
    remote = exists & ~local
    order = jnp.sum(remote[None, :] & (link[None, :] < link[:, None]), 1)
    far_rows = jnp.take(arrived, jnp.minimum(order, arrived.shape[0] - 1), axis=0)
    near_rows = jnp.take(rows, jnp.clip(link - base, 0, slots - 1), axis=0)
    return jnp.where(
        remote[:, None, None], far_rows, jnp.where(local[:, None, None], near_rows, 0.0)
    )


def shards(depth, discharge, bed, friction, tile_ids, neighbors, moves):
    slots = depth.shape[0]
    tile = depth.shape[1]
    owner_id = lax.axis_index(("gx", "gy"))
    base = owner_id * slots
    plan = moves[0]

    def local_slots(entries):
        return jnp.where(entries >= 0, entries - base, slots)

    leave_down = local_slots(plan[0, :, 0])
    leave_up = local_slots(plan[1, :, 0])
    land_low = local_slots(plan[0, :, 1])
    land_high = local_slots(plan[1, :, 1])

    def bundle(anchor):
        chosen = jnp.minimum(anchor, slots - 1)
        return jnp.concatenate(
            [
                depth[chosen][:, None],
                discharge[chosen],
                bed[chosen][:, None],
                friction[chosen][:, None],
            ],
            1,
        )

    to_low = bundle(leave_down)
    to_high = bundle(leave_up)
    framed = with_halo(jnp.stack([to_low, to_high], 0), (("gy", 0),), 1)
    from_low = framed[0]
    from_high = framed[3]
    leaving = jnp.any(
        jnp.arange(slots)[:, None] == jnp.concatenate([leave_down, leave_up])[None, :], 1
    )
    landing = jnp.concatenate([land_low, land_high])
    arrived = jnp.concatenate([from_low, from_high], 0)

    def settle(field, fresh):
        shape = (-1,) + (1,) * (field.ndim - 1)
        kept = jnp.where(leaving.reshape(shape), 0.0, field)
        return kept.at[landing].set(fresh, mode="drop")

    h = settle(depth, arrived[:, 0])
    flows = settle(discharge, arrived[:, 1:3])
    z = settle(bed, arrived[:, 3])
    fr = settle(friction, arrived[:, 4])
    qx = flows[:, 0]
    qy = flows[:, 1]
    exists = neighbors >= 0
    remote = exists & (neighbors // slots != owner_id)
    inside_x = jnp.arange(tile)[None, :, None] < tile - 1
    inside_y = jnp.arange(tile)[None, None, :] < tile - 1
    first_x = jnp.arange(tile)[None, :, None] == 0
    first_y = jnp.arange(tile)[None, None, :] == 0
    for turn in range(STEPS):
        low_rows = jnp.stack([h[:, 0, :], z[:, 0, :], fr[:, 0, :]], 1)
        left_cols = jnp.stack([h[:, :, 0], z[:, :, 0], fr[:, :, 0]], 1)
        got_above = pass_along_gx(pick_rows(low_rows, remote[:, 0], BLOCK_COLS), -1)
        got_right = pass_along_gy(pick_rows(left_cols, remote[:, 2], BLOCK_ROWS), -1)
        above = place_rows(got_above, low_rows, neighbors[:, 1], owner_id, base)
        right = place_rows(got_right, left_cols, neighbors[:, 3], owner_id, base)
        h_hi = jnp.where(inside_x, jnp.roll(h, -1, 1), above[:, 0, :][:, None, :])
        z_hi = jnp.where(inside_x, jnp.roll(z, -1, 1), above[:, 1, :][:, None, :])
        n_hi = jnp.where(inside_x, jnp.roll(fr, -1, 1), above[:, 2, :][:, None, :])
        qx_new = jnp.where(
            inside_x | exists[:, 1][:, None, None], face_flux(qx, h, h_hi, z, z_hi, fr, n_hi), 0.0
        )
        h_rt = jnp.where(inside_y, jnp.roll(h, -1, 2), right[:, 0, :][:, :, None])
        z_rt = jnp.where(inside_y, jnp.roll(z, -1, 2), right[:, 1, :][:, :, None])
        n_rt = jnp.where(inside_y, jnp.roll(fr, -1, 2), right[:, 2, :][:, :, None])
        qy_new = jnp.where(
            inside_y | exists[:, 3][:, None, None], face_flux(qy, h, h_rt, z, z_rt, fr, n_rt), 0.0
        )
        last_qx = qx_new[:, -1, :][:, None, :]
        last_qy = qy_new[:, :, -1][:, None, :]
        got_qx = pass_along_gx(pick_rows(last_qx, remote[:, 1], BLOCK_COLS), 1)
        got_qy = pass_along_gy(pick_rows(last_qy, remote[:, 3], BLOCK_ROWS), 1)
        edge_qx = place_rows(got_qx, last_qx, neighbors[:, 0], owner_id, base)[:, 0, :]
        edge_qy = place_rows(got_qy, last_qy, neighbors[:, 2], owner_id, base)[:, 0, :]
        in_x = jnp.where(first_x, edge_qx[:, None, :], jnp.roll(qx_new, 1, 1))
        in_y = jnp.where(first_y, edge_qy[:, :, None], jnp.roll(qy_new, 1, 2))
        h = h + step_time / spacing * (in_x - qx_new + (in_y - qy_new))
        qx = qx_new
        qy = qy_new
    live = (tile_ids >= 0)[:, None, None]
    new_depth = jnp.where(live, h, 0.0)
    new_discharge = jnp.stack([jnp.where(live, qx, 0.0), jnp.where(live, qy, 0.0)], 1)
    return (new_depth, new_discharge)


def solution(mesh):
    return jax.shard_map(
        shards,
        mesh=mesh,
        in_specs=(
            P(("gx", "gy"), None, None),
            P(("gx", "gy"), None, None, None),
            P(("gx", "gy"), None, None),
            P(("gx", "gy"), None, None),
            P(("gx", "gy")),
            P(("gx", "gy"), None),
            P(("gx", "gy"), None, None, None),
        ),
        out_specs=(P(("gx", "gy"), None, None), P(("gx", "gy"), None, None, None)),
        check_vma=False,
    )
```

profile of v0, /device:TPU:4, one launch (start us, length us, event | category | flops | bytes accessed | tf_op | source)
XLA Modules:
  0.0 331.5 jit_solution(9763663612857796798)
XLA Ops:
  1.4 3.1 gather_fusion.3
  4.5 3.0 gather_fusion.2
  7.4 2.8 gather_fusion.1
  11.6 3.1 maximum_bitcast_fusion
  14.7 1.9 collective-permute-start
  16.6 3.0 gather_fusion.7
  19.6 3.0 gather_fusion.6
  22.6 2.8 gather_fusion.5
  26.8 3.2 maximum_bitcast_fusion.1
  29.9 4.5 %collective-permute-start.1 = (f32[1,8,5,128,128]{4,3,2,1,0:T(8,128)}, f32[1,8,5,128,128]{4,3,2,1,0:T(8,128)}, u32[]{:S(2)}, u32[]{:S(2)}) collective-permute-start(f32[1,8,5,128,128]{4,3,2,1,0:T(8,128)} %maximum_bitcast_fusion.1), channel_id=1, source_target_pairs={{1,0},{2,1},{3,2},{4,3},{5,4},{6,5},{7,6},{9,8},{10,9},{11,10},{12... | collective-permute-start | bytes 7864328 | tf_op jit(solution)/shard_map/ppermute | solution.py:31
  37.0 5.1 %broadcast_select_fusion = f32[32,2,128,128]{3,2,1,0:T(8,128)} fusion(f32[32,2,128,128]{3,2,1,0:T(8,128)} %param.28, pred[32]{0:T(512)(128)(4,1)S(1)} %fusion.57), kind=kLoop, calls=%fused_computation.121 | loop fusion | flops 1048576 | bytes 8388640 | tf_op jit(solution)/shard_map/jit(_where)/select_n | solution.py:113
  42.1 2.8 broadcast_select_fusion.2
  44.9 16.0 %collective-permute-done = f32[1,8,5,128,128]{4,3,2,1,0:T(8,128)} collective-permute-done((f32[1,8,5,128,128]{4,3,2,1,0:T(8,128)}, f32[1,8,5,128,128]{4,3,2,1,0:T(8,128)}, u32[]{:S(2)}, u32[]{:S(2)}) %collective-permute-start) | collective-permute-done | bytes 2621472 | tf_op jit(solution)/shard_map/ppermute | solution.py:28
  60.9 14.2 %collective-permute-done.1 = f32[1,8,5,128,128]{4,3,2,1,0:T(8,128)} collective-permute-done((f32[1,8,5,128,128]{4,3,2,1,0:T(8,128)}, f32[1,8,5,128,128]{4,3,2,1,0:T(8,128)}, u32[]{:S(2)}, u32[]{:S(2)}) %collective-permute-start.1) | collective-permute-done | bytes 2621472 | tf_op jit(solution)/shard_map/ppermute | solution.py:31
  75.1 3.5 %fusion.23 = (f32[16,128,128]{2,1,0:T(8,128)S(1)}, f32[16,128,128]{2,1,0:T(8,128)}, f32[16,128,128]{2,1,0:T(8,128)}) fusion(f32[8,5,128,128]{3,2,1,0:T(8,128)} %bitcast.13, f32[8,5,128,128]{3,2,1,0:T(8,128)} %bitcast.20), kind=kLoop, calls=%fused_computation.123 | loop fusion | flops 786432 | bytes 8388608 | tf_op jit(solution)/shard_map/squeeze | solution.py:118
  78.6 3.3 scatter_fusion
  82.8 3.4 %slice_reduce_fusion.9 = (f32[32,128]{1,0:T(8,128)S(1)}, f32[32,128,1]{2,1,0:T(8,128)}) fusion(f32[32,128,128]{2,1,0:T(8,128)} %scatter_fusion), kind=kLoop, calls=%fused_computation.353 | loop fusion | bytes 49152 | tf_op jit(solution)/shard_map/jit(_roll_static)/slice | solution.py:141
  86.2 3.3 scatter_fusion.3
  90.3 3.4 %fusion.72 = (f32[32,128,1]{2,1,0:T(8,128)}, f32[32,128]{1,0:T(8,128)S(1)}) fusion(f32[32,128,128]{2,1,0:T(8,128)} %scatter_fusion.3), kind=kLoop, calls=%fused_computation.355 | loop fusion | bytes 49152 | tf_op jit(solution)/shard_map/slice | solution.py:130
  99.4 3.3 fusion
  108.7 4.9 %collective-permute-start.4 = (f32[8,3,128]{2,1,0:T(4,128)S(1)}, f32[8,3,128]{2,1,0:T(4,128)S(1)}, u32[]{:S(2)}, u32[]{:S(2)}) collective-permute-start(f32[8,3,128]{2,1,0:T(4,128)S(1)} %broadcast_select_fusion.7), channel_id=1, source_target_pairs={{1,0},{2,1},{3,2},{4,3},{5,4},{6,5},{7,6},{9,8},{10,9},{11,10},{12... | collective-permute-start | bytes 36872 | tf_op jit(solution)/shard_map/ppermute | solution.py:20
  113.6 4.2 %scatter_fusion.1 = f32[32,2,128,128]{3,2,1,0:T(8,128)} fusion(f32[32,2,128,128]{3,2,1,0:T(8,128)} %broadcast_select_fusion, s32[16]{0:T(128)S(1)} %fusion.68, f32[16,2,128,128]{3,2,1,0:T(8,128)} %fusion), kind=kCustom, calls=%fused_computation.57 | custom fusion | bytes 6291520 | tf_op jit(solution)/shard_map/scatter | solution.py:114
  118.7 6.8 %divide_select_fusion.7 = f32[32,128,128]{2,1,0:T(8,128)S(1)} fusion(f32[32,128,128]{2,1,0:T(8,128)} %scatter_fusion.3, f32[32,2,128,128]{3,2,1,0:T(8,128)} %scatter_fusion.1, f32[32,128,128]{2,1,0:T(8,128)} %scatter_fusion, f32[32,1,128]{2,1,0:T(1,128)S(1)} %slice.553, f32[32,127,128]{2,1,0:T(8,128)} %slice.552, f32[32,128]{1,0:T(8,128)S(1)} %bitcast.359, ...), kind=kLoop, calls=%fused_computation.120 | loop fusion | flops 12582912 | bytes 16830592 | tf_op jit(solution)/shard_map/jit(_where)/select_n | solution.py:138
  127.5 4.4 %collective-permute-start.3 = (f32[4,1,128]{2,0,1:T(4,128)S(1)}, f32[4,1,128]{2,0,1:T(4,128)S(1)}, u32[]{:S(2)}, u32[]{:S(2)}) collective-permute-start(f32[4,1,128]{2,0,1:T(4,128)S(1)} %bitcast_select_fusion.23), channel_id=1, source_target_pairs={{0,8},{8,16},{16,24},{1,9},{9,17},{17,25},{2,10},{10,18},{18,26},{... | collective-permute-start | bytes 6152 | tf_op jit(solution)/shard_map/ppermute | solution.py:20
  131.9 3.5 %slice.566 = f32[32,128,127]{2,1,0:T(8,128)} slice(f32[32,128,128]{2,1,0:T(8,128)} %scatter_fusion), slice={[0:32], [0:128], [1:128]} | slice | bytes 4161536 | tf_op jit(solution)/shard_map/jit(_roll_static)/slice | solution.py:141
  137.4 1.9 slice.573
  142.0 9.7 %divide_select_fusion.6 = (f32[32,128,128]{2,1,0:T(8,128)S(1)}, f32[32,128,128]{2,1,0:T(8,128)}, f32[32,128,128]{2,1,0:T(8,128)}) fusion(f32[32,128,128]{2,1,0:T(8,128)} %scatter_fusion.3, f32[32,2,128,128]{3,2,1,0:T(8,128)} %scatter_fusion.1, f32[32,128,128]{2,1,0:T(8,128)} %scatter_fusion, f32[32,128,1]{2,1,0:T(8,128)} %get-tuple-element.85, ...), kind=kLoop, calls=%fused_computation.119 | loop fusion | flops 12582912 | bytes 21024896 | tf_op jit(solution)/shard_map/jit(_where)/select_n | solution.py:144
  151.7 2.0 slice_reduce_fusion.6
  156.9 3.2 collective-permute-done.5
  160.8 5.5 %fusion.4 = f32[32,128,128]{2,1,0:T(8,128)S(1)} fusion(f32[32,128,128]{2,1,0:T(8,128)} %scatter_fusion, f32[32,128,128]{2,1,0:T(8,128)} %copy-done.10, f32[32,127,128]{2,1,0:T(8,128)} %bitcast.298, f32[32,1,128]{2,1,0:T(1,128)S(1)} %slice.563, f32[32,128,128]{2,1,0:T(8,128)} %copy-done.8, f32[32,128,127]{2,1,0:T(8,128)} %bitcast.296, ...), kind=kLoop, calls=%fused_computation.77 | loop fusion | flops 4718592 | bytes 12615808 | tf_op jit(solution)/shard_map/add | solution.py:155
  166.4 2.0 slice_reduce_fusion.5
  171.1 3.1 slice.577
  174.9 1.9 collective-permute-start.8
  177.7 6.7 %divide_select_fusion.5 = f32[32,128,128]{2,1,0:T(8,128)S(1)} fusion(f32[32,128,128]{2,1,0:T(8,128)} %copy-done.10, f32[32,128,128]{2,1,0:T(8,128)} %scatter_fusion.3, f32[32,128,128]{2,1,0:T(8,128)} %copy-done.5, f32[32,1,128]{2,1,0:T(1,128)S(1)} %slice.578, f32[32,127,128]{2,1,0:T(8,128)} %slice.577, f32[32,128]{1,0:T(8,128)S(1)} %bitcast.353, ...), kind=kLoop, calls=%fused_computation.118 | loop fusion | flops 12582912 | bytes 16830592 | tf_op jit(solution)/shard_map/jit(_where)/select_n | solution.py:138
  186.5 4.5 %collective-permute-start.7 = (f32[4,1,128]{2,0,1:T(4,128)S(1)}, f32[4,1,128]{2,0,1:T(4,128)S(1)}, u32[]{:S(2)}, u32[]{:S(2)}) collective-permute-start(f32[4,1,128]{2,0,1:T(4,128)S(1)} %bitcast_select_fusion.22), channel_id=1, source_target_pairs={{0,8},{8,16},{16,24},{1,9},{9,17},{17,25},{2,10},{10,18},{18,26},{... | collective-permute-start | bytes 6152 | tf_op jit(solution)/shard_map/ppermute | solution.py:20
  191.0 3.5 %slice.584 = f32[32,128,127]{2,1,0:T(8,128)} slice(f32[32,128,128]{2,1,0:T(8,128)} %copy-done.5), slice={[0:32], [0:128], [1:128]} | slice | bytes 4161536 | tf_op jit(solution)/shard_map/jit(_roll_static)/slice | solution.py:141
  197.2 6.6 %divide_select_fusion.4 = f32[32,128,128]{2,1,0:T(8,128)S(1)} fusion(f32[32,128,128]{2,1,0:T(8,128)} %copy-done.8, f32[32,128,128]{2,1,0:T(8,128)} %scatter_fusion.3, f32[32,128,128]{2,1,0:T(8,128)} %get-tuple-element.46, f32[32,128,128]{2,1,0:T(8,128)} %get-tuple-element.45, f32[32,128,128]{2,1,0:T(8,128)} %copy-done.5, ...), kind=kLoop, calls=%fused_computation.117 | loop fusion | flops 11534336 | bytes 16830592 | tf_op jit(solution)/shard_map/jit(_where)/select_n | solution.py:144
  203.8 2.0 slice_reduce_fusion.4
  206.5 2.3 collective-permute-start.9
  209.5 2.8 collective-permute-done.9
  212.9 5.5 %fusion.9 = f32[32,128,128]{2,1,0:T(8,128)S(1)} fusion(f32[32,128,128]{2,1,0:T(8,128)} %copy-done.5, f32[32,128,128]{2,1,0:T(8,128)} %copy-done.12, f32[32,127,128]{2,1,0:T(8,128)} %bitcast.300, f32[32,1,128]{2,1,0:T(1,128)S(1)} %slice.582, f32[32,128,128]{2,1,0:T(8,128)} %copy-done.9, f32[32,128,127]{2,1,0:T(8,128)} %bitcast.297, ...), kind=kLoop, calls=%fused_computation.88 | loop fusion | flops 4718592 | bytes 12615808 | tf_op jit(solution)/shard_map/add | solution.py:155
  218.4 1.9 slice_reduce_fusion.3
  223.1 3.2 slice.591
  226.8 1.9 collective-permute-start.12
  229.6 6.7 %divide_select_fusion.3 = f32[32,128,128]{2,1,0:T(8,128)S(1)} fusion(f32[32,128,128]{2,1,0:T(8,128)} %copy-done.12, f32[32,128,128]{2,1,0:T(8,128)} %scatter_fusion.3, f32[32,128,128]{2,1,0:T(8,128)} %copy-done.6, f32[32,1,128]{2,1,0:T(1,128)S(1)} %slice.592, f32[32,127,128]{2,1,0:T(8,128)} %slice.591, f32[32,128]{1,0:T(8,128)S(1)} %bitcast.356, ...), kind=kLoop, calls=%fused_computation.116 | loop fusion | flops 12582912 | bytes 16830592 | tf_op jit(solution)/shard_map/jit(_where)/select_n | solution.py:138
  238.4 4.5 %collective-permute-start.11 = (f32[4,1,128]{2,0,1:T(4,128)S(1)}, f32[4,1,128]{2,0,1:T(4,128)S(1)}, u32[]{:S(2)}, u32[]{:S(2)}) collective-permute-start(f32[4,1,128]{2,0,1:T(4,128)S(1)} %bitcast_select_fusion.21), channel_id=1, source_target_pairs={{0,8},{8,16},{16,24},{1,9},{9,17},{17,25},{2,10},{10,18},{18,26},{... | collective-permute-start | bytes 6152 | tf_op jit(solution)/shard_map/ppermute | solution.py:20
  243.0 3.6 %slice.598 = f32[32,128,127]{2,1,0:T(8,128)} slice(f32[32,128,128]{2,1,0:T(8,128)} %copy-done.6), slice={[0:32], [0:128], [1:128]} | slice | bytes 4161536 | tf_op jit(solution)/shard_map/jit(_roll_static)/slice | solution.py:141
  249.2 6.6 %divide_select_fusion.2 = f32[32,128,128]{2,1,0:T(8,128)S(1)} fusion(f32[32,128,128]{2,1,0:T(8,128)} %copy-done.9, f32[32,128,128]{2,1,0:T(8,128)} %scatter_fusion.3, f32[32,128,128]{2,1,0:T(8,128)} %get-tuple-element.46, f32[32,128,128]{2,1,0:T(8,128)} %get-tuple-element.45, f32[32,128,128]{2,1,0:T(8,128)} %copy-done.6, ...), kind=kLoop, calls=%fused_computation.115 | loop fusion | flops 11534336 | bytes 16830592 | tf_op jit(solution)/shard_map/jit(_where)/select_n | solution.py:144
  255.8 2.1 slice_reduce_fusion.2
  258.5 2.1 collective-permute-start.13
  261.3 3.0 collective-permute-done.13
  265.0 5.6 %fusion.14 = f32[32,128,128]{2,1,0:T(8,128)S(1)} fusion(f32[32,128,128]{2,1,0:T(8,128)} %copy-done.6, f32[32,128,128]{2,1,0:T(8,128)} %copy-done.11, f32[32,127,128]{2,1,0:T(8,128)} %bitcast.299, f32[32,1,128]{2,1,0:T(1,128)S(1)} %slice.596, f32[32,128,128]{2,1,0:T(8,128)} %copy-done.7, f32[32,128,127]{2,1,0:T(8,128)} %bitcast.295, ...), kind=kLoop, calls=%fused_computation.97 | loop fusion | flops 4718592 | bytes 12615808 | tf_op jit(solution)/shard_map/add | solution.py:155
  270.6 2.0 fusion.71
  275.3 3.1 slice.605
  279.9 7.4 %select_bitcast_fusion.1 = (f32[32,1,128,128]{3,2,0,1:T(8,128)}, f32[32,128,128]{2,1,0:T(8,128)S(1)}) fusion(pred[32]{0:T(512)(128)(4,1)S(1)} %broadcast_compare_fusion.1, f32[32,128,128]{2,1,0:T(8,128)} %copy-done.11, f32[32,128,128]{2,1,0:T(8,128)} %scatter_fusion.3, f32[32,128]{1,0:T(8,128)S(1)} %bitcast.344, f32[32,1,128]{2,1,0:T(1,128)S(1)} %slice.557, ...), kind=kLoop, calls=%fused_computation.112 | loop fusion | flops 13107200 | bytes 18927776 | tf_op jit(solution)/shard_map/stack | solution.py:160
  289.3 4.5 %collective-permute-start.15 = (f32[4,1,128]{2,0,1:T(4,128)S(1)}, f32[4,1,128]{2,0,1:T(4,128)S(1)}, u32[]{:S(2)}, u32[]{:S(2)}) collective-permute-start(f32[4,1,128]{2,0,1:T(4,128)S(1)} %bitcast_select_fusion.20), channel_id=1, source_target_pairs={{0,8},{8,16},{16,24},{1,9},{9,17},{17,25},{2,10},{10,18},{18,26},{... | collective-permute-start | bytes 6152 | tf_op jit(solution)/shard_map/ppermute | solution.py:20
  294.5 3.6 %slice.612 = f32[32,128,127]{2,1,0:T(8,128)} slice(f32[32,128,128]{2,1,0:T(8,128)} %copy-done.3), slice={[0:32], [0:128], [1:128]} | slice | bytes 4161536 | tf_op jit(solution)/shard_map/jit(_roll_static)/slice | solution.py:141
  298.1 2.2 collective-permute-start.16
  302.4 7.8 %select_bitcast_fusion = (f32[32,1,128,128]{3,2,0,1:T(8,128)}, f32[32,128,128]{2,1,0:T(8,128)S(1)}) fusion(pred[32]{0:T(512)(128)(4,1)S(1)} %broadcast_compare_fusion.1, f32[32,128,128]{2,1,0:T(8,128)} %copy-done.7, f32[32,128,128]{2,1,0:T(8,128)} %scatter_fusion.3, f32[32,128,128]{2,1,0:T(8,128)} %get-tuple-element.46, f32[32,128]{1,0:T(8,128)S(1)} %bitcast.338, ...), kind=kLoop, calls=%fused_computation.111 | loop fusion | flops 12058624 | bytes 18927776 | tf_op jit(solution)/shard_map/stack | solution.py:160
  310.1 2.0 slice_reduce_fusion
  312.9 2.4 collective-permute-start.17
  315.3 3.9 %pad_maximum_fusion = f32[32,2,128,128]{3,2,0,1:T(8,128)} fusion(f32[32,1,128,128]{3,2,0,1:T(8,128)S(1)} %copy-done.15, f32[32,1,128,128]{3,2,0,1:T(8,128)} %get-tuple-element.28), kind=kLoop, calls=%fused_computation.64 | loop fusion | flops 1048576 | bytes 8388608 | tf_op jit(solution)/shard_map/stack | solution.py:160
  319.8 4.8 %copy.265 = f32[32,2,128,128]{3,2,1,0:T(8,128)} copy(f32[32,2,128,128]{3,2,0,1:T(8,128)} %pad_maximum_fusion) | data formatting | bytes 8388608
  325.3 6.2 %fusion.20 = f32[32,128,128]{2,1,0:T(8,128)} fusion(f32[32,128,128]{2,1,0:T(8,128)S(1)} %copy-done.4, f32[32,128,128]{2,1,0:T(8,128)} %copy-done.14, f32[32,127,128]{2,1,0:T(8,128)} %bitcast.302, f32[32,1,128]{2,1,0:T(1,128)S(1)} %slice.610, f32[32,128,128]{2,1,0:T(8,128)} %copy-done.13, f32[32,128,127]{2,1,0:T(8,128)} %bitcast.301, ...), kind=kLoop, calls=%fused_computation.107 | loop fusion | flops 5242880 | bytes 12615840 | tf_op jit(solution)/shard_map/jit(_where)/select_n | solution.py:159
  (233 shorter events, 62.8 us)
Async XLA Ops:
  1.4 8.9 %copy-start.18 = (f32[32,128,128]{2,1,0:T(8,128)S(1)}, f32[32,128,128]{2,1,0:T(8,128)}, u32[]{:S(2)}) copy-start(f32[32,128,128]{2,1,0:T(8,128)} %param.27) | copy-start | bytes 6291460
  14.7 46.2 %collective-permute-start = (f32[1,8,5,128,128]{4,3,2,1,0:T(8,128)}, f32[1,8,5,128,128]{4,3,2,1,0:T(8,128)}, u32[]{:S(2)}, u32[]{:S(2)}) collective-permute-start(f32[1,8,5,128,128]{4,3,2,1,0:T(8,128)} %maximum_bitcast_fusion), channel_id=1, source_target_pairs={{0,1},{1,2},{2,3},{3,4},{4,5},{5,6},{6,7},{8,9},{9,10},{10,11},{11... | collective-permute-start | bytes 7864328 | tf_op jit(solution)/shard_map/ppermute | solution.py:28
  26.8 7.7 %copy-start.21 = (s32[1,2,8,2]{2,3,1,0:T(2,128)S(1)}, s32[1,2,8,2]{2,3,1,0:T(2,128)}, u32[]{:S(2)}) copy-start(s32[1,2,8,2]{2,3,1,0:T(2,128)} %param.33) | copy-start | bytes 388
  26.8 7.7 %copy-start.20 = (s32[32,4]{0,1:T(4,128)S(1)}, s32[32,4]{0,1:T(4,128)}, u32[]{:S(2)}) copy-start(s32[32,4]{0,1:T(4,128)} %param.32) | copy-start | bytes 1540
  29.9 45.2 %collective-permute-start.1 = (f32[1,8,5,128,128]{4,3,2,1,0:T(8,128)}, f32[1,8,5,128,128]{4,3,2,1,0:T(8,128)}, u32[]{:S(2)}, u32[]{:S(2)}) collective-permute-start(f32[1,8,5,128,128]{4,3,2,1,0:T(8,128)} %maximum_bitcast_fusion.1), channel_id=1, source_target_pairs={{1,0},{2,1},{3,2},{4,3},{5,4},{6,5},{7,6},{9,8},{10,9},{11,10},{12... | collective-permute-start | bytes 7864328 | tf_op jit(solution)/shard_map/ppermute | solution.py:31
  37.0 5.1 %copy-start.16 = (f32[32,128,128]{2,1,0:T(8,128)S(1)}, f32[32,128,128]{2,1,0:T(8,128)}, u32[]{:S(2)}) copy-start(f32[32,128,128]{2,1,0:T(8,128)} %param.29) | copy-start | bytes 6291460
  37.0 5.1 %copy-start.17 = (f32[32,128,128]{2,1,0:T(8,128)S(1)}, f32[32,128,128]{2,1,0:T(8,128)}, u32[]{:S(2)}) copy-start(f32[32,128,128]{2,1,0:T(8,128)} %param.30) | copy-start | bytes 6291460
  37.0 5.1 %copy-start.19 = (f32[32,128,128]{2,1,0:T(8,128)S(1)}, f32[32,128,128]{2,1,0:T(8,128)}, u32[]{:S(2)}) copy-start(f32[32,128,128]{2,1,0:T(8,128)} %param.27) | copy-start | bytes 6291460
  97.4 20.4 %collective-permute-start.2 = (f32[4,3,128]{2,1,0:T(4,128)S(1)}, f32[4,3,128]{2,1,0:T(4,128)S(1)}, u32[]{:S(2)}, u32[]{:S(2)}) collective-permute-start(f32[4,3,128]{2,1,0:T(4,128)S(1)} %broadcast_select_fusion.11), channel_id=1, source_target_pairs={{8,0},{16,8},{24,16},{9,1},{17,9},{25,17},{10,2},{18,10},{26,18},{... | collective-permute-start | bytes 18440 | tf_op jit(solution)/shard_map/ppermute | solution.py:20
  99.4 3.3 copy-start.2
  102.7 2.3 copy-start
  108.7 32.4 %collective-permute-start.4 = (f32[8,3,128]{2,1,0:T(4,128)S(1)}, f32[8,3,128]{2,1,0:T(4,128)S(1)}, u32[]{:S(2)}, u32[]{:S(2)}) collective-permute-start(f32[8,3,128]{2,1,0:T(4,128)S(1)} %broadcast_select_fusion.7), channel_id=1, source_target_pairs={{1,0},{2,1},{3,2},{4,3},{5,4},{6,5},{7,6},{9,8},{10,9},{11,10},{12... | collective-permute-start | bytes 36872 | tf_op jit(solution)/shard_map/ppermute | solution.py:20
  125.4 1.4 copy-start.10
  127.5 13.0 %collective-permute-start.3 = (f32[4,1,128]{2,0,1:T(4,128)S(1)}, f32[4,1,128]{2,0,1:T(4,128)S(1)}, u32[]{:S(2)}, u32[]{:S(2)}) collective-permute-start(f32[4,1,128]{2,0,1:T(4,128)S(1)} %bitcast_select_fusion.23), channel_id=1, source_target_pairs={{0,8},{8,16},{16,24},{1,9},{9,17},{17,25},{2,10},{10,18},{18,26},{... | collective-permute-start | bytes 6152 | tf_op jit(solution)/shard_map/ppermute | solution.py:20
  135.5 1.9 copy-start.1
  151.7 2.0 copy-start.8
  154.3 5.8 %collective-permute-start.5 = (f32[8,1,128]{2,0,1:T(8,128)S(1)}, f32[8,1,128]{2,0,1:T(8,128)S(1)}, u32[]{:S(2)}, u32[]{:S(2)}) collective-permute-start(f32[8,1,128]{2,0,1:T(8,128)S(1)} %bitcast_select_fusion.19), channel_id=1, source_target_pairs={{0,1},{1,2},{2,3},{3,4},{4,5},{5,6},{6,7},{8,9},{9,10},{10,11},{11... | collective-permute-start | bytes 12296 | tf_op jit(solution)/shard_map/ppermute | solution.py:20
  166.4 2.1 copy-start.5
  169.1 7.7 %collective-permute-start.6 = (f32[4,3,128]{2,1,0:T(4,128)S(1)}, f32[4,3,128]{2,1,0:T(4,128)S(1)}, u32[]{:S(2)}, u32[]{:S(2)}) collective-permute-start(f32[4,3,128]{2,1,0:T(4,128)S(1)} %broadcast_select_fusion.10), channel_id=1, source_target_pairs={{8,0},{16,8},{24,16},{9,1},{17,9},{25,17},{10,2},{18,10},{26,18},{... | collective-permute-start | bytes 18440 | tf_op jit(solution)/shard_map/ppermute | solution.py:20
  174.9 21.4 %collective-permute-start.8 = (f32[8,3,128]{2,1,0:T(4,128)S(1)}, f32[8,3,128]{2,1,0:T(4,128)S(1)}, u32[]{:S(2)}, u32[]{:S(2)}) collective-permute-start(f32[8,3,128]{2,1,0:T(4,128)S(1)} %broadcast_select_fusion.6), channel_id=1, source_target_pairs={{1,0},{2,1},{3,2},{4,3},{5,4},{6,5},{7,6},{9,8},{10,9},{11,10},{12... | collective-permute-start | bytes 36872 | tf_op jit(solution)/shard_map/ppermute | solution.py:20
  184.4 1.4 copy-start.12
  186.5 9.3 %collective-permute-start.7 = (f32[4,1,128]{2,0,1:T(4,128)S(1)}, f32[4,1,128]{2,0,1:T(4,128)S(1)}, u32[]{:S(2)}, u32[]{:S(2)}) collective-permute-start(f32[4,1,128]{2,0,1:T(4,128)S(1)} %bitcast_select_fusion.22), channel_id=1, source_target_pairs={{0,8},{8,16},{16,24},{1,9},{9,17},{17,25},{2,10},{10,18},{18,26},{... | collective-permute-start | bytes 6152 | tf_op jit(solution)/shard_map/ppermute | solution.py:20
  203.8 2.1 copy-start.9
  206.5 5.8 %collective-permute-start.9 = (f32[8,1,128]{2,0,1:T(8,128)S(1)}, f32[8,1,128]{2,0,1:T(8,128)S(1)}, u32[]{:S(2)}, u32[]{:S(2)}) collective-permute-start(f32[8,1,128]{2,0,1:T(8,128)S(1)} %bitcast_select_fusion.18), channel_id=1, source_target_pairs={{0,1},{1,2},{2,3},{3,4},{4,5},{5,6},{6,7},{8,9},{9,10},{10,11},{11... | collective-permute-start | bytes 12296 | tf_op jit(solution)/shard_map/ppermute | solution.py:20
  218.4 2.0 copy-start.6
  221.1 7.7 %collective-permute-start.10 = (f32[4,3,128]{2,1,0:T(4,128)S(1)}, f32[4,3,128]{2,1,0:T(4,128)S(1)}, u32[]{:S(2)}, u32[]{:S(2)}) collective-permute-start(f32[4,3,128]{2,1,0:T(4,128)S(1)} %broadcast_select_fusion.9), channel_id=1, source_target_pairs={{8,0},{16,8},{24,16},{9,1},{17,9},{25,17},{10,2},{18,10},{26,18},{... | collective-permute-start | bytes 18440 | tf_op jit(solution)/shard_map/ppermute | solution.py:20
  226.8 21.5 %collective-permute-start.12 = (f32[8,3,128]{2,1,0:T(4,128)S(1)}, f32[8,3,128]{2,1,0:T(4,128)S(1)}, u32[]{:S(2)}, u32[]{:S(2)}) collective-permute-start(f32[8,3,128]{2,1,0:T(4,128)S(1)} %broadcast_select_fusion.5), channel_id=1, source_target_pairs={{1,0},{2,1},{3,2},{4,3},{5,4},{6,5},{7,6},{9,8},{10,9},{11,10},{12... | collective-permute-start | bytes 36872 | tf_op jit(solution)/shard_map/ppermute | solution.py:20
  229.6 13.3 %copy-start.22 = (s32[32]{0:T(128)S(1)}, s32[32]{0:T(128)}, u32[]{:S(2)}) copy-start(s32[32]{0:T(128)} %param.31) | copy-start | bytes 388
  236.4 1.4 copy-start.11
  238.4 9.3 %collective-permute-start.11 = (f32[4,1,128]{2,0,1:T(4,128)S(1)}, f32[4,1,128]{2,0,1:T(4,128)S(1)}, u32[]{:S(2)}, u32[]{:S(2)}) collective-permute-start(f32[4,1,128]{2,0,1:T(4,128)S(1)} %bitcast_select_fusion.21), channel_id=1, source_target_pairs={{0,8},{8,16},{16,24},{1,9},{9,17},{17,25},{2,10},{10,18},{18,26},{... | collective-permute-start | bytes 6152 | tf_op jit(solution)/shard_map/ppermute | solution.py:20
  255.8 2.1 copy-start.7
  258.5 5.8 %collective-permute-start.13 = (f32[8,1,128]{2,0,1:T(8,128)S(1)}, f32[8,1,128]{2,0,1:T(8,128)S(1)}, u32[]{:S(2)}, u32[]{:S(2)}) collective-permute-start(f32[8,1,128]{2,0,1:T(8,128)S(1)} %bitcast_select_fusion.17), channel_id=1, source_target_pairs={{0,1},{1,2},{2,3},{3,4},{4,5},{5,6},{6,7},{8,9},{9,10},{10,11},{11... | collective-permute-start | bytes 12296 | tf_op jit(solution)/shard_map/ppermute | solution.py:20
  270.6 2.1 copy-start.3
  273.4 5.7 %collective-permute-start.14 = (f32[4,3,128]{2,1,0:T(4,128)S(1)}, f32[4,3,128]{2,1,0:T(4,128)S(1)}, u32[]{:S(2)}, u32[]{:S(2)}) collective-permute-start(f32[4,3,128]{2,1,0:T(4,128)S(1)} %broadcast_select_fusion.8), channel_id=1, source_target_pairs={{8,0},{16,8},{24,16},{9,1},{17,9},{25,17},{10,2},{18,10},{26,18},{... | collective-permute-start | bytes 18440 | tf_op jit(solution)/shard_map/ppermute | solution.py:20
  287.3 1.4 copy-start.14
  289.3 11.5 %collective-permute-start.15 = (f32[4,1,128]{2,0,1:T(4,128)S(1)}, f32[4,1,128]{2,0,1:T(4,128)S(1)}, u32[]{:S(2)}, u32[]{:S(2)}) collective-permute-start(f32[4,1,128]{2,0,1:T(4,128)S(1)} %bitcast_select_fusion.20), channel_id=1, source_target_pairs={{0,8},{8,16},{16,24},{1,9},{9,17},{17,25},{2,10},{10,18},{18,26},{... | collective-permute-start | bytes 6152 | tf_op jit(solution)/shard_map/ppermute | solution.py:20
  298.1 3.4 %collective-permute-start.16 = (f32[8,3,128]{2,1,0:T(4,128)S(1)}, f32[8,3,128]{2,1,0:T(4,128)S(1)}, u32[]{:S(2)}, u32[]{:S(2)}) collective-permute-start(f32[8,3,128]{2,1,0:T(4,128)S(1)} %broadcast_select_fusion.4), channel_id=1, source_target_pairs={{1,0},{2,1},{3,2},{4,3},{5,4},{6,5},{7,6},{9,8},{10,9},{11,10},{12... | collective-permute-start | bytes 36872 | tf_op jit(solution)/shard_map/ppermute | solution.py:20
  310.1 2.1 copy-start.13
  310.1 5.2 %copy-start.15 = (f32[32,1,128,128]{3,2,0,1:T(8,128)S(1)}, f32[32,1,128,128]{3,2,0,1:T(8,128)}, u32[]{:S(2)}) copy-start(f32[32,1,128,128]{3,2,0,1:T(8,128)} %get-tuple-element.30) | copy-start | bytes 6291460
  312.9 11.7 %collective-permute-start.17 = (f32[8,1,128]{2,0,1:T(8,128)S(1)}, f32[8,1,128]{2,0,1:T(8,128)S(1)}, u32[]{:S(2)}, u32[]{:S(2)}) collective-permute-start(f32[8,1,128]{2,0,1:T(8,128)S(1)} %bitcast_select_fusion.16), channel_id=1, source_target_pairs={{0,1},{1,2},{2,3},{3,4},{4,5},{5,6},{6,7},{8,9},{9,10},{10,11},{11... | collective-permute-start | bytes 12296 | tf_op jit(solution)/shard_map/ppermute | solution.py:20
  319.8 5.5 %copy-start.4 = (f32[32,128,128]{2,1,0:T(8,128)S(1)}, f32[32,128,128]{2,1,0:T(8,128)}, u32[]{:S(2)}) copy-start(f32[32,128,128]{2,1,0:T(8,128)} %copy-done.3) | copy-start | bytes 6291460
where the time goes:
time: 334 us; the launch traced here: 332 us
  local copies, waits for them, and re-layouts  129 us (39%)
  other arithmetic  112 us (34%)
  starting transfers between devices  49.3 us (15%)
  waiting for transfers between devices  39.3 us (12%)
    ppermute x16, starting transfers between devices, shifted(): return lax.ppermute(block, axis, route)  42.9 us
    slice x12, local copies, waits for them, and re-layouts, shards(): h_rt = jnp.where(inside_y, jnp.roll(h, -1, 2), right[:, 0, :][:, :, None])  23.7 us
    select_n x3, other arithmetic, shards(): jnp.where(inside_y | exists[:, 3][:, None, None], face_flux(qy, h, h_rt,...  22.9 us
    select_n x3, other arithmetic, shards(): jnp.where(inside_x | exists[:, 1][:, None, None], face_flux(qx, h, h_hi,...  20.2 us
    another operation x3, other arithmetic, shards(): jnp.stack([jnp.where(live, qx, 0.0), jnp.where(live, qy, 0.0)], 1)  19 us
    add x3, other arithmetic, shards(): h = h + step_time / spacing * (in_x - qx_new + (in_y - qy_new))  16.6 us
    ppermute x1, waiting for transfers between devices, with_halo(): lax.ppermute(lax.slice_in_dim(block, block.shape[dim] - width, None, axis...  16 us
    ppermute x1, waiting for transfers between devices, with_halo(): lax.ppermute(lax.slice_in_dim(block, 0, width, axis=dim), axis, backward)  14.2 us
  transfers between devices with their start and end apart: 18, of which 5 were waited for; matrix products, arithmetic and copies ran while one was open for 34% of the time, Pallas kernels for 0%

commit v1 on v0

v1 whole, which is shorter than its diff:
```python
import functools

import jax
import jax.numpy as jnp
from jax import lax
from jax.experimental import pallas as pl
from jax.experimental.pallas import tpu as pltpu
from jax.sharding import PartitionSpec as P

BLOCK_ROWS = 8
BLOCK_COLS = 4
STEPS = 4

gravity = 9.81
step_time = 0.25
spacing = 2.0
min_depth = 0.15

F32 = jnp.float32
COUNTS = (BLOCK_COLS, BLOCK_COLS, BLOCK_ROWS, BLOCK_ROWS)
OPPOSITE = (1, 0, 3, 2)


def neighbour(block, axis, shift):
    count = lax.axis_size(axis)
    route = [(i + shift, i) for i in range(count) if 0 <= i + shift < count]
    return lax.ppermute(block, axis, route)


def face(q, depth_sum, rise, rough):
    d = jnp.maximum(0.5 * depth_sum, min_depth)
    drive = q - (gravity * step_time / spacing) * d * rise
    power = jnp.exp2(-(7.0 / 3.0) * jnp.log2(d))
    return drive / (1.0 + (gravity * step_time * 0.5) * rough * jnp.abs(q) * power)


def eye_of(tile):
    return lax.broadcasted_iota(jnp.int32, (tile, tile), 0) == lax.broadcasted_iota(
        jnp.int32, (tile, tile), 1
    )


def as_row(column, eye):
    return jnp.sum(jnp.where(eye, column, 0.0), 0, keepdims=True)


def as_column(row, eye):
    return jnp.sum(jnp.where(eye, row, 0.0), 1, keepdims=True)


def store_edges(ref, at, slot, x, eye):
    tile = x.shape[0]
    ref[at, pl.ds(slot, 1), :] = x[:1]
    ref[at + 1, pl.ds(slot, 1), :] = x[tile - 1 :]
    ref[at + 2, pl.ds(slot, 1), :] = as_row(x[:, :1], eye)
    ref[at + 3, pl.ds(slot, 1), :] = as_row(x[:, tile - 1 :], eye)


def fill_sends(pick_ref, edge_ref, send_refs, kinds):
    for side in range(4):
        for m in range(COUNTS[side]):
            slot = pick_ref[side, m]
            for j, kind in enumerate(kinds[side]):
                send_refs[side][j, m : m + 1, :] = edge_ref[kind, pl.ds(slot, 1), :]


FIRST_KINDS = ((0, 4, 8), (1, 5, 9, 12), (2, 6, 10), (3, 7, 11, 13))
LATER_KINDS = ((0,), (1,), (2,), (3,))


def bundle_kernel(down, up, *refs):
    ins, outs = refs[:8], refs[8:]
    for way in range(2):
        h, q, z, n = ins[4 * way : 4 * way + 4]
        out = outs[way]
        out[0, 0] = h[0]
        out[0, 1] = q[0, 0]
        out[0, 2] = q[0, 1]
        out[0, 3] = z[0]
        out[0, 4] = n[0]


def bundle(down, up, depth, discharge, bed, friction):
    tile = depth.shape[1]
    movers = down.shape[0]

    def one(which):
        return pl.BlockSpec((1, tile, tile), lambda m, d, u: ((d, u)[which][m], 0, 0))

    def two(which):
        return pl.BlockSpec((1, 2, tile, tile), lambda m, d, u: ((d, u)[which][m], 0, 0, 0))

    out = pl.BlockSpec((1, 5, tile, tile), lambda m, d, u: (m, 0, 0, 0))
    shape = jax.ShapeDtypeStruct((movers, 5, tile, tile), F32)
    return pl.pallas_call(
        bundle_kernel,
        grid_spec=pltpu.PrefetchScalarGridSpec(
            num_scalar_prefetch=2,
            grid=(movers,),
            in_specs=[one(0), two(0), one(0), one(0), one(1), two(1), one(1), one(1)],
            out_specs=[out, out],
        ),
        out_shape=[shape, shape],
        name="bundle",
    )(down, up, depth, discharge, bed, friction, depth, discharge, bed, friction)


def settle_kernel(mode, own, low, high, pick, *refs):
    h, q, z, n, lo, hi, ho, qo, zo, no, edges, s0, s1, s2, s3 = refs
    slot = pl.program_id(0)
    kind = mode[slot]

    @pl.when(kind == 0)
    def _():
        ho[...] = h[...]
        qo[...] = q[...]
        zo[...] = z[...]
        no[...] = n[...]

    def take(src):
        ho[0] = src[0, 0]
        qo[0, 0] = src[0, 1]
        qo[0, 1] = src[0, 2]
        zo[0] = src[0, 3]
        no[0] = src[0, 4]

    pl.when(kind == 1)(lambda: take(lo))
    pl.when(kind == 2)(lambda: take(hi))

    @pl.when(kind == 3)
    def _():
        for ref in (ho, qo, zo, no):
            ref[...] = jnp.zeros_like(ref)

    tile = h.shape[1]
    eye = eye_of(tile)
    store_edges(edges, 0, slot, ho[0], eye)
    store_edges(edges, 4, slot, zo[0], eye)
    store_edges(edges, 8, slot, no[0], eye)
    edges[12, pl.ds(slot, 1), :] = qo[0, 0, tile - 1 :, :]
    edges[13, pl.ds(slot, 1), :] = as_row(qo[0, 1][:, tile - 1 :], eye)

    @pl.when(slot == pl.num_programs(0) - 1)
    def _():
        fill_sends(pick, edges, (s0, s1, s2, s3), FIRST_KINDS)


def whole(shape):
    return pl.BlockSpec(shape, lambda *_: (0,) * len(shape))


def settle(mode, own, low, high, pick, depth, discharge, bed, friction, got_low, got_high):
    slots, tile = depth.shape[:2]
    one = pl.BlockSpec((1, tile, tile), lambda s, m, o, l, h, p: (o[s], 0, 0))
    two = pl.BlockSpec((1, 2, tile, tile), lambda s, m, o, l, h, p: (o[s], 0, 0, 0))
    lo = pl.BlockSpec((1, 5, tile, tile), lambda s, m, o, l, h, p: (l[s], 0, 0, 0))
    hi = pl.BlockSpec((1, 5, tile, tile), lambda s, m, o, l, h, p: (h[s], 0, 0, 0))
    out1 = pl.BlockSpec((1, tile, tile), lambda s, *_: (s, 0, 0))
    out2 = pl.BlockSpec((1, 2, tile, tile), lambda s, *_: (s, 0, 0, 0))
    sends = [(len(k), c, tile) for k, c in zip(FIRST_KINDS, COUNTS)]
    small = [(14, slots, tile)] + sends
    return pl.pallas_call(
        settle_kernel,
        grid_spec=pltpu.PrefetchScalarGridSpec(
            num_scalar_prefetch=5,
            grid=(slots,),
            in_specs=[one, two, one, one, lo, hi],
            out_specs=[out1, out2, out1, out1] + [whole(s) for s in small],
        ),
        out_shape=[
            jax.ShapeDtypeStruct(x.shape, F32) for x in (depth, discharge, bed, friction)
        ]
        + [jax.ShapeDtypeStruct(s, F32) for s in small],
        name="settle",
    )(mode, own, low, high, pick, depth, discharge, bed, friction, got_low, got_high)


def edge_fluxes(first, link, edges, gots, static, halo, flux):
    slots = halo.shape[1]

    def gather(side, kind, j, at):
        got = gots[side]
        count = got.shape[1]

        def body(s, _):
            k = link[side, s]
            near = edges[kind, pl.ds(jnp.clip(k, 0, slots - 1), 1), :]
            far = got[j, pl.ds(jnp.clip(k - slots, 0, count - 1), 1), :]
            row = jnp.where(k >= slots, far, near)
            halo[at, pl.ds(s, 1), :] = jnp.where(k >= 0, row, 0.0)
            return 0

        lax.fori_loop(0, slots, body, 0, unroll=8)

    q_old, rise_z, rough = static
    for side in range(4):
        other = OPPOSITE[side]
        gather(side, other, 0, 0)
        if first:
            gather(side, 4 + other, 1, 1)
            gather(side, 8 + other, 2, 2)
            dz = halo[1] - edges[4 + side]
            rise_z[side] = dz if side % 2 else -dz
            rough[side] = halo[2] + edges[8 + side]
            if side % 2:
                q = edges[12 + side // 2]
            else:
                gather(side, 12 + side // 2, 3, 3)
                q = halo[3]
        else:
            q = q_old[side]
        own = edges[side]
        dh = halo[0] - own
        rise = (dh if side % 2 else -dh) + rise_z[side]
        flux[side] = face(q, halo[0] + own, rise, rough[side])


def step_kernel(first, last, link, pick, live, *refs):
    refs = list(refs)

    def pop(count):
        out, refs[:count] = refs[:count], []
        return out

    h_ref, q_ref, z_ref, n_ref, edges = pop(5)
    gots = pop(4)
    if first:
        walls = pop(1)[0]
    else:
        q_old, rise_in, rough_in, walls = pop(4)
    ho, qo = pop(2)
    if not last:
        edges_out, s0, s1, s2, s3, flux = pop(6)
        if first:
            rise_out, rough_out = pop(2)
    else:
        flux = pop(1)[0]
        if first:
            rise_out, rough_out = pop(2)
    halo = pop(1)[0]
    slot = pl.program_id(0)
    static = (None, rise_out, rough_out) if first else (q_old, rise_in, rough_in)

    @pl.when(slot == 0)
    def _():
        edge_fluxes(first, link, edges, gots, static, halo, flux)
        flux[...] = jnp.where(walls[...] >= 0, flux[...], 0.0)

    h, z, n = h_ref[0], z_ref[0], n_ref[0]
    tile = h.shape[0]
    eye = eye_of(tile)
    row_id = lax.broadcasted_iota(jnp.int32, (tile, tile), 0)
    col_id = lax.broadcasted_iota(jnp.int32, (tile, tile), 1)
    w = h + z

    def along(dim, q, index, in_edge, out_edge):
        nxt = functools.partial(pltpu.roll, shift=tile - 1, axis=dim)
        flow = face(q, h + nxt(h), nxt(w) - w, n + nxt(n))
        flow = jnp.where(index == tile - 1, out_edge, flow)
        inflow = jnp.where(index == 0, in_edge, pltpu.roll(flow, 1, dim))
        return flow, inflow

    def edge(side):
        return flux[side, pl.ds(slot, 1), :]

    qx, in_x = along(0, q_ref[0, 0], row_id, edge(0), edge(1))
    qy, in_y = along(
        1, q_ref[0, 1], col_id, as_column(edge(2), eye), as_column(edge(3), eye)
    )
    h = h + (step_time / spacing) * ((in_x - qx) + (in_y - qy))
    if last:
        keep = live[slot] >= 0
        h = jnp.where(keep, h, 0.0)
        qx = jnp.where(keep, qx, 0.0)
        qy = jnp.where(keep, qy, 0.0)
    ho[0] = h
    qo[0, 0] = qx
    qo[0, 1] = qy
    if not last:
        store_edges(edges_out, 0, slot, h, eye)

        @pl.when(slot == pl.num_programs(0) - 1)
        def _():
            fill_sends(pick, edges_out, (s0, s1, s2, s3), LATER_KINDS)


def step(first, last, link, pick, live, state, edges, gots, static, walls):
    h, q, z, n = state
    slots, tile = h.shape[:2]
    one = pl.BlockSpec((1, tile, tile), lambda s, *_: (s, 0, 0))
    two = pl.BlockSpec((1, 2, tile, tile), lambda s, *_: (s, 0, 0, 0))
    table = (4, slots, tile)
    smalls_in = [edges, *gots, *static, walls]
    out_small = []
    if not last:
        out_small += [table] + [(len(k), c, tile) for k, c in zip(LATER_KINDS, COUNTS)]
    out_small += [table]
    if first:
        out_small += [table, table]
    return pl.pallas_call(
        functools.partial(step_kernel, first, last),
        grid_spec=pltpu.PrefetchScalarGridSpec(
            num_scalar_prefetch=3,
            grid=(slots,),
            in_specs=[one, two, one, one] + [whole(x.shape) for x in smalls_in],
            out_specs=[one, two] + [whole(s) for s in out_small],
            scratch_shapes=[pltpu.VMEM((4, slots, tile), F32)],
        ),
        out_shape=[jax.ShapeDtypeStruct(h.shape, F32), jax.ShapeDtypeStruct(q.shape, F32)]
        + [jax.ShapeDtypeStruct(s, F32) for s in out_small],
        name="step",
    )(link, pick, live, h, q, z, n, *smalls_in)


def exchange(sends):
    return [
        neighbour(sends[1], "gx", -1),
        neighbour(sends[0], "gx", 1),
        neighbour(sends[3], "gy", -1),
        neighbour(sends[2], "gy", 1),
    ]


def shards(depth, discharge, bed, friction, tile_ids, neighbors, moves):
    slots, tile = depth.shape[:2]
    owner_id = lax.axis_index("gx") * lax.axis_size("gy") + lax.axis_index("gy")
    base = owner_id * slots
    plan = moves[0]
    slot_id = jnp.arange(slots)

    leave = jnp.where(plan[:, :, 0] >= 0, plan[:, :, 0] - base, slots)
    land = jnp.where(plan[:, :, 1] >= 0, plan[:, :, 1] - base, slots)
    chosen = jnp.minimum(leave, slots - 1)
    to_low, to_high = bundle(chosen[0], chosen[1], depth, discharge, bed, friction)
    from_low = neighbour(to_high, "gy", -1)
    from_high = neighbour(to_low, "gy", 1)

    left = jnp.any(slot_id[:, None, None] == leave[None], (1, 2))
    lands = slot_id[:, None, None] == land[None]
    arrive = jnp.any(lands, 2)
    movers = plan.shape[1]
    entry = jnp.sum(jnp.where(lands, jnp.arange(movers)[None, None], 0), 2)
    mode = jnp.where(arrive[:, 0], 1, jnp.where(arrive[:, 1], 2, jnp.where(left, 3, 0)))

    def carried(used, value):
        seen = jnp.max(
            jnp.where(used[None] & (slot_id[None] <= slot_id[:, None]), slot_id[None], -1), 1
        )
        return jnp.sum(jnp.where(seen[:, None] == slot_id[None], value[None], 0), 1)

    own = carried(mode == 0, slot_id)
    low = carried(arrive[:, 0], entry[:, 0])
    high = carried(arrive[:, 1], entry[:, 1])

    links = neighbors.T
    remote = (links >= 0) & (links // slots != owner_id)
    rank = jnp.sum(remote[:, None, :] & (links[:, None, :] < links[:, :, None]), 2)
    link = jnp.where(remote, slots + rank, jnp.where(links >= 0, links - base, -1))
    before = jnp.sum(remote[:, None, :] & (slot_id[None, None] < slot_id[None, :, None]), 2)
    hit = remote[:, None, :] & (before[:, None, :] == jnp.arange(BLOCK_ROWS)[None, :, None])
    pick = jnp.sum(jnp.where(hit, slot_id[None, None], 0), 2)
    walls = jnp.broadcast_to(links[:, :, None], (4, slots, tile))
    as_int = lambda *xs: [x.astype(jnp.int32) for x in xs]
    mode, own, low, high, link, pick = as_int(mode, own, low, high, link, pick)

    h, q, z, n, edges, *sends = settle(
        mode, own, low, high, pick, depth, discharge, bed, friction, from_low, from_high
    )
    static = ()
    for turn in range(STEPS):
        first, last = turn == 0, turn == STEPS - 1
        gots = exchange(sends)
        h, q, *rest = step(
            first, last, link, pick, tile_ids, (h, q, z, n), edges, gots, static, walls
        )
        if not last:
            edges, *sends = rest[:5]
            rest = rest[5:]
        static = (rest[0],) + (tuple(rest[1:3]) if first else static[1:])
    return h, q


def solution(mesh):
    return jax.shard_map(
        shards,
        mesh=mesh,
        in_specs=(
            P(("gx", "gy"), None, None),
            P(("gx", "gy"), None, None, None),
            P(("gx", "gy"), None, None),
            P(("gx", "gy"), None, None),
            P(("gx", "gy")),
            P(("gx", "gy"), None),
            P(("gx", "gy"), None, None, None),
        ),
        out_specs=(P(("gx", "gy"), None, None), P(("gx", "gy"), None, None, None)),
        check_vma=False,
    )
```

time: 334 us -> 271 us (0.81)
  Pallas kernels: 0 us -> 141 us
  local copies, waits for them, and re-layouts: 129 us -> 3.36 us
  other arithmetic: 112 us -> 5.53 us
  waiting for transfers between devices: 39.3 us -> 66.1 us
    pallas_call x0 -> x6, Pallas kernels: none -> 141 us  [the longest x4 110 us: step(): pl.pallas_call(functools.partial(step_kernel, first, last), grid_spec=plt...]
    select_n x39 -> x2, other arithmetic: 60.8 us -> 1.32 us  [the longest x1 0.76 us: shards(): land = jnp.where(plan[:, :, 1] >= 0, plan[:, :, 1] - base, slots)]
    slice x40 -> x0, local copies, waits for them, and re-layouts: 57 us -> none  [the longest x12 23.7 us: shards(): h_rt = jnp.where(inside_y, jnp.roll(h, -1, 2), right[:, 0, :][:, :, None])]
    gather x56 -> x0, local copies, waits for them, and re-layouts: 48.3 us -> none  [the longest x16 9.46 us: place_rows(): near_rows = jnp.take(rows, jnp.clip(link - base, 0, slots - 1), axis=0)]
    ppermute x18, waiting for transfers between devices: 39.3 us -> 66.1 us  [neighbour(): return lax.ppermute(block, axis, route)]
    another operation x17 -> x0, other arithmetic: 25.9 us -> none  [the longest x3 19 us: shards(): jnp.stack([jnp.where(live, qx, 0.0), jnp.where(live, qy, 0.0)], 1)]
    add x3 -> x0, other arithmetic: 16.6 us -> none  [shards(): h = h + step_time / spacing * (in_x - qx_new + (in_y - qy_new))]
    scatter x4 -> x0, local copies, waits for them, and re-layouts: 11.8 us -> none  [settle(): return kept.at[landing].set(fresh, mode='drop')]
  transfers between devices with their start and end apart: 18 -> 18, of which waited for: 5 -> 9; matrix products, arithmetic and copies ran while one was open for 34% -> 2% of each run, Pallas kernels for 0% -> 0%
where the time goes in v1:
time: 271 us; the launch traced here: 267 us
  Pallas kernels  141 us (52%)
  waiting for transfers between devices  66.1 us (24%)
  starting transfers between devices  50.1 us (18%)
  other arithmetic  5.53 us (2%)
  local copies, waits for them, and re-layouts  3.36 us (1%)
    pallas_call x4, Pallas kernels, step(): pl.pallas_call(functools.partial(step_kernel, first, last), grid_spec=plt...  110 us
    ppermute x18, waiting for transfers between devices, neighbour(): return lax.ppermute(block, axis, route)  66.1 us
    ppermute x18, starting transfers between devices, neighbour(): return lax.ppermute(block, axis, route)  50.1 us
    pallas_call x1, Pallas kernels, settle(): pl.pallas_call(settle_kernel, grid_spec=pltpu.PrefetchScalarGridSpec(num_...  23.5 us
    pallas_call x1, Pallas kernels, bundle(): pl.pallas_call(bundle_kernel, grid_spec=pltpu.PrefetchScalarGridSpec(num_...  7.54 us
  transfers between devices with their start and end apart: 18, of which 9 were waited for; matrix products, arithmetic and copies ran while one was open for 2% of the time, Pallas kernels for 0%

profile of v1, /device:TPU:4, one launch (start us, length us, event | category | flops | bytes accessed | tf_op | source)
XLA Modules:
  0.0 267.1 jit_solution(5745909550704447972)
XLA Ops:
  0.6 0.8 compare_select_fusion.1
  1.4 0.5 slice_bitcast_fusion.2
  1.9 7.5 %bundle.1 = (f32[8,5,128,128]{3,2,1,0:T(8,128)}, f32[8,5,128,128]{3,2,1,0:T(8,128)}) custom-call(s32[8]{0:T(128)} %get-tuple-element.87.down, s32[8]{0:T(128)} %get-tuple-element.86.up, f32[32,128,128]{2,1,0:T(8,128)} %refs_0_.3, f32[32,2,128,128]{3,2,1,0:T(8,128)} %refs_1_.3, f32[32,128,128]{2,1,0:T(8,128)} %refs_2_.3, f32[32,128,128]{2,1,0:T(8,128)} %refs_3_.3, ...), custom_call_target="tpu_custom_call" | custom-call | tf_op jit(solution)/shard_map/bundle/pallas_call | solution.py:95
  9.5 1.9 collective-permute-start
  11.4 4.5 %collective-permute-start.1 = (f32[8,5,128,128]{3,2,1,0:T(8,128)}, f32[8,5,128,128]{3,2,1,0:T(8,128)}, u32[]{:S(2)}, u32[]{:S(2)}) collective-permute-start(f32[8,5,128,128]{3,2,1,0:T(8,128)} %get-tuple-element.42), channel_id=1, source_target_pairs={{1,0},{2,1},{3,2},{4,3},{5,4},{6,5},{7,6},{9,8},{10,9},{11,10},{12... | collective-permute-start | bytes 7864328 | tf_op jit(solution)/shard_map/ppermute | solution.py:27
  15.9 0.1 fusion.4
  16.0 0.5 broadcast_compare_fusion.1
  16.5 0.1 select_reduce_fusion.5
  16.7 0.1 select_reduce_fusion.1
  16.8 0.1 select_reduce_fusion.3
  16.9 0.3 convert_reduce_fusion
  17.2 0.7 select_reduce_fusion.6.pick
  17.9 0.7 select_reduce_fusion.4.own
  18.6 0.1 select_reduce_fusion.7
  18.7 0.7 select_reduce_fusion.high
  19.4 0.8 select_reduce_fusion.2.low
  20.2 48.4 %collective-permute-done.refs_4_ = f32[8,5,128,128]{3,2,1,0:T(8,128)S(1)} collective-permute-done((f32[8,5,128,128]{3,2,1,0:T(8,128)}, f32[8,5,128,128]{3,2,1,0:T(8,128)S(1)}, u32[]{:S(2)}, u32[]{:S(2)}) %collective-permute-start) | collective-permute-done | bytes 2621472 | tf_op jit(solution)/shard_map/ppermute | solution.py:27
  68.6 1.1 collective-permute-done.1.refs_5_
  69.7 0.4 copy-done
  70.1 23.5 %settle.1 = (f32[32,128,128]{2,1,0:T(8,128)}, f32[32,2,128,128]{3,2,1,0:T(8,128)}, f32[32,128,128]{2,1,0:T(8,128)}, f32[32,128,128]{2,1,0:T(8,128)}, f32[14,32,1...) custom-call(s32[32]{0:T(128)} %get-tuple-element.83.mode, ...), custom_call_target="tpu_custom_call" | custom-call | tf_op jit(solution)/shard_map/settle/pallas_call | solution.py:162
  93.6 1.3 collective-permute-start.3
  94.9 4.6 %collective-permute-start.2 = (f32[4,4,128]{2,1,0:T(4,128)}, f32[4,4,128]{2,1,0:T(4,128)S(1)}, u32[]{:S(2)}, u32[]{:S(2)}) collective-permute-start(f32[4,4,128]{2,1,0:T(4,128)} %get-tuple-element.48), channel_id=1, source_target_pairs={{0,8},{8,16},{16,24},{1,9},{9,17},{17,25},{2,10},{10,18},{18,26},{... | collective-permute-start | bytes 24584 | tf_op jit(solution)/shard_map/ppermute | solution.py:27
  99.5 3.7 %collective-permute-start.5 = (f32[3,8,128]{2,1,0:T(8,128)}, f32[3,8,128]{2,1,0:T(8,128)S(1)}, u32[]{:S(2)}, u32[]{:S(2)}) collective-permute-start(f32[3,8,128]{2,1,0:T(8,128)} %get-tuple-element.51), channel_id=1, source_target_pairs={{1,0},{2,1},{3,2},{4,3},{5,4},{6,5},{7,6},{9,8},{10,9},{11,10},{12... | collective-permute-start | bytes 36872 | tf_op jit(solution)/shard_map/ppermute | solution.py:27
  103.2 1.9 collective-permute-start.4
  105.2 0.6 select_select_fusion.link
  105.7 0.0 collective-permute-done.3.refs_6_
  105.8 0.0 collective-permute-done.5.refs_8_
  105.8 3.6 %collective-permute-done.4.refs_7_ = f32[4,8,128]{2,1,0:T(8,128)S(1)} collective-permute-done((f32[4,8,128]{2,1,0:T(8,128)}, f32[4,8,128]{2,1,0:T(8,128)S(1)}, u32[]{:S(2)}, u32[]{:S(2)}) %collective-permute-start.4) | collective-permute-done | bytes 16416 | tf_op jit(solution)/shard_map/ppermute | solution.py:27
  109.4 0.7 broadcast_in_dim.139.refs_9_.refs_12_
  110.1 30.3 %step.4 = (f32[32,128,128]{2,1,0:T(8,128)}, f32[32,2,128,128]{3,2,1,0:T(8,128)}, f32[4,32,128]{2,1,0:T(8,128)}, f32[1,4,128]{2,1,0:T(4,128)}, f32[1,4,128]{2,1,0...) custom-call(s32[4,32]{1,0:T(4,128)} %select_select_fusion.link, ...), custom_call_target="tpu_custom_call" | custom-call | tf_op jit(solution)/shard_map/step/pallas_call | solution.py:300
  140.5 1.9 collective-permute-start.8
  142.4 4.5 %collective-permute-start.9 = (f32[1,8,128]{2,1,0:T(8,128)}, f32[1,8,128]{2,1,0:T(8,128)S(1)}, u32[]{:S(2)}, u32[]{:S(2)}) collective-permute-start(f32[1,8,128]{2,1,0:T(8,128)} %get-tuple-element.58), channel_id=1, source_target_pairs={{1,0},{2,1},{3,2},{4,3},{5,4},{6,5},{7,6},{9,8},{10,9},{11,10},{12... | collective-permute-start | bytes 12296 | tf_op jit(solution)/shard_map/ppermute | solution.py:27
  147.0 3.3 %collective-permute-start.6 = (f32[1,4,128]{2,1,0:T(4,128)}, f32[1,4,128]{2,1,0:T(4,128)S(1)}, u32[]{:S(2)}, u32[]{:S(2)}) collective-permute-start(f32[1,4,128]{2,1,0:T(4,128)} %get-tuple-element.55), channel_id=1, source_target_pairs={{0,8},{8,16},{16,24},{1,9},{9,17},{17,25},{2,10},{10,18},{18,26},{... | collective-permute-start | bytes 6152 | tf_op jit(solution)/shard_map/ppermute | solution.py:27
  150.3 1.3 collective-permute-start.7
  151.6 0.2 collective-permute-done.6.refs_5_
  151.8 4.2 %collective-permute-done.7.refs_6_ = f32[1,4,128]{2,1,0:T(4,128)S(1)} collective-permute-done((f32[1,4,128]{2,1,0:T(4,128)}, f32[1,4,128]{2,1,0:T(4,128)S(1)}, u32[]{:S(2)}, u32[]{:S(2)}) %collective-permute-start.7) | collective-permute-done | bytes 2080 | tf_op jit(solution)/shard_map/ppermute | solution.py:27
  156.0 0.0 collective-permute-done.8.refs_7_
  156.0 0.0 collective-permute-done.9.refs_8_
  156.0 0.6 copy-done.16
  156.6 0.0 copy-done.7
  156.6 0.0 copy-done.10
  156.6 28.1 %step.5 = (f32[32,128,128]{2,1,0:T(8,128)}, f32[32,2,128,128]{3,2,1,0:T(8,128)}, f32[4,32,128]{2,1,0:T(8,128)}, f32[1,4,128]{2,1,0:T(4,128)}, f32[1,4,128]{2,1,0...) custom-call(s32[4,32]{1,0:T(4,128)} %select_select_fusion.link, ...), custom_call_target="tpu_custom_call" | custom-call | tf_op jit(solution)/shard_map/step/pallas_call | solution.py:300
  184.7 1.9 collective-permute-start.12
  186.6 4.5 %collective-permute-start.13 = (f32[1,8,128]{2,1,0:T(8,128)}, f32[1,8,128]{2,1,0:T(8,128)S(1)}, u32[]{:S(2)}, u32[]{:S(2)}) collective-permute-start(f32[1,8,128]{2,1,0:T(8,128)} %get-tuple-element.68), channel_id=1, source_target_pairs={{1,0},{2,1},{3,2},{4,3},{5,4},{6,5},{7,6},{9,8},{10,9},{11,10},{12... | collective-permute-start | bytes 12296 | tf_op jit(solution)/shard_map/ppermute | solution.py:27
  191.1 3.5 %collective-permute-start.10 = (f32[1,4,128]{2,1,0:T(4,128)}, f32[1,4,128]{2,1,0:T(4,128)S(1)}, u32[]{:S(2)}, u32[]{:S(2)}) collective-permute-start(f32[1,4,128]{2,1,0:T(4,128)} %get-tuple-element.65), channel_id=1, source_target_pairs={{0,8},{8,16},{16,24},{1,9},{9,17},{17,25},{2,10},{10,18},{18,26},{... | collective-permute-start | bytes 6152 | tf_op jit(solution)/shard_map/ppermute | solution.py:27
  194.7 1.3 collective-permute-start.11
  196.0 0.2 collective-permute-done.10.refs_5_
  196.2 4.0 %collective-permute-done.11.refs_6_ = f32[1,4,128]{2,1,0:T(4,128)S(1)} collective-permute-done((f32[1,4,128]{2,1,0:T(4,128)}, f32[1,4,128]{2,1,0:T(4,128)S(1)}, u32[]{:S(2)}, u32[]{:S(2)}) %collective-permute-start.11) | collective-permute-done | bytes 2080 | tf_op jit(solution)/shard_map/ppermute | solution.py:27
  200.2 0.0 collective-permute-done.12.refs_7_
  200.2 0.0 collective-permute-done.13.refs_8_
  200.3 0.6 copy-done.17
  200.8 0.0 copy-done.8
  200.8 0.0 copy-done.11
  200.8 28.1 %step.6 = (f32[32,128,128]{2,1,0:T(8,128)}, f32[32,2,128,128]{3,2,1,0:T(8,128)}, f32[4,32,128]{2,1,0:T(8,128)}, f32[1,4,128]{2,1,0:T(4,128)}, f32[1,4,128]{2,1,0...) custom-call(s32[4,32]{1,0:T(4,128)} %select_select_fusion.link, ...), custom_call_target="tpu_custom_call" | custom-call | tf_op jit(solution)/shard_map/step/pallas_call | solution.py:300
  228.9 1.9 collective-permute-start.16
  230.8 4.5 %collective-permute-start.17 = (f32[1,8,128]{2,1,0:T(8,128)}, f32[1,8,128]{2,1,0:T(8,128)S(1)}, u32[]{:S(2)}, u32[]{:S(2)}) collective-permute-start(f32[1,8,128]{2,1,0:T(8,128)} %get-tuple-element.76), channel_id=1, source_target_pairs={{1,0},{2,1},{3,2},{4,3},{5,4},{6,5},{7,6},{9,8},{10,9},{11,10},{12... | collective-permute-start | bytes 12296 | tf_op jit(solution)/shard_map/ppermute | solution.py:27
  235.4 1.9 collective-permute-start.14
  237.3 1.3 collective-permute-start.15
  238.6 0.2 collective-permute-done.14.refs_5_
  238.8 4.0 %collective-permute-done.15.refs_6_ = f32[1,4,128]{2,1,0:T(4,128)S(1)} collective-permute-done((f32[1,4,128]{2,1,0:T(4,128)}, f32[1,4,128]{2,1,0:T(4,128)S(1)}, u32[]{:S(2)}, u32[]{:S(2)}) %collective-permute-start.15) | collective-permute-done | bytes 2080 | tf_op jit(solution)/shard_map/ppermute | solution.py:27
  242.9 0.5 copy-done.15
  243.4 0.0 copy-done.6
  243.5 0.0 copy-done.9
  243.5 23.6 %step.7 = (f32[32,128,128]{2,1,0:T(8,128)}, f32[32,2,128,128]{3,2,1,0:T(8,128)}, f32[4,32,128]{2,1,0:T(8,128)}) custom-call(s32[4,32]{1,0:T(4,128)} %select_select_fusion.link, s32[4,8]{1,0:T(4,128)} %select_reduce_fusion.6.pick, s32[32]{0:T(128)} %live.7, f32[32,128,128]{2,1,0:T(8,128)} %get-tuple-element.70.refs_0_, ...), custom_call_target="tpu_custom_call" | custom-call | tf_op jit(solution)/shard_map/step/pallas_call | solution.py:300
  (34 shorter events, 0.1 us)
Async XLA Ops:
  1.9 15.0 %copy-start.1 = (s32[32,4]{0,1:T(4,128)S(1)}, s32[32,4]{0,1:T(4,128)}, u32[]{:S(2)}) copy-start(s32[32,4]{0,1:T(4,128)} %param.12) | copy-start | bytes 1540
  9.5 59.1 %collective-permute-start = (f32[8,5,128,128]{3,2,1,0:T(8,128)}, f32[8,5,128,128]{3,2,1,0:T(8,128)S(1)}, u32[]{:S(2)}, u32[]{:S(2)}) collective-permute-start(f32[8,5,128,128]{3,2,1,0:T(8,128)} %get-tuple-element.41), channel_id=1, source_target_pairs={{0,1},{1,2},{2,3},{3,4},{4,5},{5,6},{6,7},{8,9},{9,10},{10,11},{11... | collective-permute-start | bytes 7864328 | tf_op jit(solution)/shard_map/ppermute | solution.py:27
  11.4 58.4 %collective-permute-start.1 = (f32[8,5,128,128]{3,2,1,0:T(8,128)}, f32[8,5,128,128]{3,2,1,0:T(8,128)}, u32[]{:S(2)}, u32[]{:S(2)}) collective-permute-start(f32[8,5,128,128]{3,2,1,0:T(8,128)} %get-tuple-element.42), channel_id=1, source_target_pairs={{1,0},{2,1},{3,2},{4,3},{5,4},{6,5},{7,6},{9,8},{10,9},{11,10},{12... | collective-permute-start | bytes 7864328 | tf_op jit(solution)/shard_map/ppermute | solution.py:27
  68.6 1.5 copy-start
  93.6 12.1 %collective-permute-start.3 = (f32[3,4,128]{2,1,0:T(4,128)}, f32[3,4,128]{2,1,0:T(4,128)S(1)}, u32[]{:S(2)}, u32[]{:S(2)}) collective-permute-start(f32[3,4,128]{2,1,0:T(4,128)} %get-tuple-element.49), channel_id=1, source_target_pairs={{8,0},{16,8},{24,16},{9,1},{17,9},{25,17},{10,2},{18,10},{26,18},{... | collective-permute-start | bytes 18440 | tf_op jit(solution)/shard_map/ppermute | solution.py:27
  94.9 10.8 %collective-permute-start.2 = (f32[4,4,128]{2,1,0:T(4,128)}, f32[4,4,128]{2,1,0:T(4,128)S(1)}, u32[]{:S(2)}, u32[]{:S(2)}) collective-permute-start(f32[4,4,128]{2,1,0:T(4,128)} %get-tuple-element.48), channel_id=1, source_target_pairs={{0,8},{8,16},{16,24},{1,9},{9,17},{17,25},{2,10},{10,18},{18,26},{... | collective-permute-start | bytes 24584 | tf_op jit(solution)/shard_map/ppermute | solution.py:27
  99.5 6.2 %collective-permute-start.5 = (f32[3,8,128]{2,1,0:T(8,128)}, f32[3,8,128]{2,1,0:T(8,128)S(1)}, u32[]{:S(2)}, u32[]{:S(2)}) collective-permute-start(f32[3,8,128]{2,1,0:T(8,128)} %get-tuple-element.51), channel_id=1, source_target_pairs={{1,0},{2,1},{3,2},{4,3},{5,4},{6,5},{7,6},{9,8},{10,9},{11,10},{12... | collective-permute-start | bytes 36872 | tf_op jit(solution)/shard_map/ppermute | solution.py:27
  103.2 6.2 %collective-permute-start.4 = (f32[4,8,128]{2,1,0:T(8,128)}, f32[4,8,128]{2,1,0:T(8,128)S(1)}, u32[]{:S(2)}, u32[]{:S(2)}) collective-permute-start(f32[4,8,128]{2,1,0:T(8,128)} %get-tuple-element.50), channel_id=1, source_target_pairs={{0,1},{1,2},{2,3},{3,4},{4,5},{5,6},{6,7},{8,9},{9,10},{10,11},{11... | collective-permute-start | bytes 49160 | tf_op jit(solution)/shard_map/ppermute | solution.py:27
  105.7 4.4 %copy-start.5 = (f32[3,4,128]{2,1,0:T(4,128)}, f32[3,4,128]{2,1,0:T(4,128)S(1)}, u32[]{:S(2)}) copy-start(f32[3,4,128]{2,1,0:T(4,128)S(1)} %collective-permute-done.3.refs_6_) | copy-start | bytes 18436
  105.7 4.4 %copy-start.4 = (f32[4,4,128]{2,1,0:T(4,128)}, f32[4,4,128]{2,1,0:T(4,128)S(1)}, u32[]{:S(2)}) copy-start(f32[4,4,128]{2,1,0:T(4,128)S(1)} %collective-permute-done.2.refs_5_) | copy-start | bytes 24580
  105.8 4.4 %copy-start.3 = (f32[3,8,128]{2,1,0:T(8,128)}, f32[3,8,128]{2,1,0:T(8,128)S(1)}, u32[]{:S(2)}) copy-start(f32[3,8,128]{2,1,0:T(8,128)S(1)} %collective-permute-done.5.refs_8_) | copy-start | bytes 36868
  109.4 0.7 copy-start.2
  140.5 15.5 %collective-permute-start.8 = (f32[1,8,128]{2,1,0:T(8,128)}, f32[1,8,128]{2,1,0:T(8,128)S(1)}, u32[]{:S(2)}, u32[]{:S(2)}) collective-permute-start(f32[1,8,128]{2,1,0:T(8,128)} %get-tuple-element.57), channel_id=1, source_target_pairs={{0,1},{1,2},{2,3},{3,4},{4,5},{5,6},{6,7},{8,9},{9,10},{10,11},{11... | collective-permute-start | bytes 12296 | tf_op jit(solution)/shard_map/ppermute | solution.py:27
  142.4 13.6 %collective-permute-start.9 = (f32[1,8,128]{2,1,0:T(8,128)}, f32[1,8,128]{2,1,0:T(8,128)S(1)}, u32[]{:S(2)}, u32[]{:S(2)}) collective-permute-start(f32[1,8,128]{2,1,0:T(8,128)} %get-tuple-element.58), channel_id=1, source_target_pairs={{1,0},{2,1},{3,2},{4,3},{5,4},{6,5},{7,6},{9,8},{10,9},{11,10},{12... | collective-permute-start | bytes 12296 | tf_op jit(solution)/shard_map/ppermute | solution.py:27
  147.0 4.9 %collective-permute-start.6 = (f32[1,4,128]{2,1,0:T(4,128)}, f32[1,4,128]{2,1,0:T(4,128)S(1)}, u32[]{:S(2)}, u32[]{:S(2)}) collective-permute-start(f32[1,4,128]{2,1,0:T(4,128)} %get-tuple-element.55), channel_id=1, source_target_pairs={{0,8},{8,16},{16,24},{1,9},{9,17},{17,25},{2,10},{10,18},{18,26},{... | collective-permute-start | bytes 6152 | tf_op jit(solution)/shard_map/ppermute | solution.py:27
  150.3 5.7 %collective-permute-start.7 = (f32[1,4,128]{2,1,0:T(4,128)}, f32[1,4,128]{2,1,0:T(4,128)S(1)}, u32[]{:S(2)}, u32[]{:S(2)}) collective-permute-start(f32[1,4,128]{2,1,0:T(4,128)} %get-tuple-element.56), channel_id=1, source_target_pairs={{8,0},{16,8},{24,16},{9,1},{17,9},{25,17},{10,2},{18,10},{26,18},{... | collective-permute-start | bytes 6152 | tf_op jit(solution)/shard_map/ppermute | solution.py:27
  151.8 4.2 %copy-start.13 = (f32[1,4,128]{2,1,0:T(4,128)}, f32[1,4,128]{2,1,0:T(4,128)S(1)}, u32[]{:S(2)}) copy-start(f32[1,4,128]{2,1,0:T(4,128)S(1)} %collective-permute-done.6.refs_5_) | copy-start | bytes 6148
  156.0 0.6 copy-start.16
  156.0 0.6 copy-start.7
  156.0 0.6 copy-start.10
  184.7 15.6 %collective-permute-start.12 = (f32[1,8,128]{2,1,0:T(8,128)}, f32[1,8,128]{2,1,0:T(8,128)S(1)}, u32[]{:S(2)}, u32[]{:S(2)}) collective-permute-start(f32[1,8,128]{2,1,0:T(8,128)} %get-tuple-element.67), channel_id=1, source_target_pairs={{0,1},{1,2},{2,3},{3,4},{4,5},{5,6},{6,7},{8,9},{9,10},{10,11},{11... | collective-permute-start | bytes 12296 | tf_op jit(solution)/shard_map/ppermute | solution.py:27
  186.6 13.6 %collective-permute-start.13 = (f32[1,8,128]{2,1,0:T(8,128)}, f32[1,8,128]{2,1,0:T(8,128)S(1)}, u32[]{:S(2)}, u32[]{:S(2)}) collective-permute-start(f32[1,8,128]{2,1,0:T(8,128)} %get-tuple-element.68), channel_id=1, source_target_pairs={{1,0},{2,1},{3,2},{4,3},{5,4},{6,5},{7,6},{9,8},{10,9},{11,10},{12... | collective-permute-start | bytes 12296 | tf_op jit(solution)/shard_map/ppermute | solution.py:27
  191.1 5.1 %collective-permute-start.10 = (f32[1,4,128]{2,1,0:T(4,128)}, f32[1,4,128]{2,1,0:T(4,128)S(1)}, u32[]{:S(2)}, u32[]{:S(2)}) collective-permute-start(f32[1,4,128]{2,1,0:T(4,128)} %get-tuple-element.65), channel_id=1, source_target_pairs={{0,8},{8,16},{16,24},{1,9},{9,17},{17,25},{2,10},{10,18},{18,26},{... | collective-permute-start | bytes 6152 | tf_op jit(solution)/shard_map/ppermute | solution.py:27
  194.7 5.5 %collective-permute-start.11 = (f32[1,4,128]{2,1,0:T(4,128)}, f32[1,4,128]{2,1,0:T(4,128)S(1)}, u32[]{:S(2)}, u32[]{:S(2)}) collective-permute-start(f32[1,4,128]{2,1,0:T(4,128)} %get-tuple-element.66), channel_id=1, source_target_pairs={{8,0},{16,8},{24,16},{9,1},{17,9},{25,17},{10,2},{18,10},{26,18},{... | collective-permute-start | bytes 6152 | tf_op jit(solution)/shard_map/ppermute | solution.py:27
  196.2 4.1 %copy-start.14 = (f32[1,4,128]{2,1,0:T(4,128)}, f32[1,4,128]{2,1,0:T(4,128)S(1)}, u32[]{:S(2)}) copy-start(f32[1,4,128]{2,1,0:T(4,128)S(1)} %collective-permute-done.10.refs_5_) | copy-start | bytes 6148
  200.2 0.6 copy-start.17
  200.2 0.6 copy-start.8
  200.2 0.6 copy-start.11
  228.9 13.9 %collective-permute-start.16 = (f32[1,8,128]{2,1,0:T(8,128)}, f32[1,8,128]{2,1,0:T(8,128)S(1)}, u32[]{:S(2)}, u32[]{:S(2)}) collective-permute-start(f32[1,8,128]{2,1,0:T(8,128)} %get-tuple-element.75), channel_id=1, source_target_pairs={{0,1},{1,2},{2,3},{3,4},{4,5},{5,6},{6,7},{8,9},{9,10},{10,11},{11... | collective-permute-start | bytes 12296 | tf_op jit(solution)/shard_map/ppermute | solution.py:27
  230.8 12.0 %collective-permute-start.17 = (f32[1,8,128]{2,1,0:T(8,128)}, f32[1,8,128]{2,1,0:T(8,128)S(1)}, u32[]{:S(2)}, u32[]{:S(2)}) collective-permute-start(f32[1,8,128]{2,1,0:T(8,128)} %get-tuple-element.76), channel_id=1, source_target_pairs={{1,0},{2,1},{3,2},{4,3},{5,4},{6,5},{7,6},{9,8},{10,9},{11,10},{12... | collective-permute-start | bytes 12296 | tf_op jit(solution)/shard_map/ppermute | solution.py:27
  235.4 3.4 %collective-permute-start.14 = (f32[1,4,128]{2,1,0:T(4,128)}, f32[1,4,128]{2,1,0:T(4,128)S(1)}, u32[]{:S(2)}, u32[]{:S(2)}) collective-permute-start(f32[1,4,128]{2,1,0:T(4,128)} %get-tuple-element.73), channel_id=1, source_target_pairs={{0,8},{8,16},{16,24},{1,9},{9,17},{17,25},{2,10},{10,18},{18,26},{... | collective-permute-start | bytes 6152 | tf_op jit(solution)/shard_map/ppermute | solution.py:27
  237.3 5.5 %collective-permute-start.15 = (f32[1,4,128]{2,1,0:T(4,128)}, f32[1,4,128]{2,1,0:T(4,128)S(1)}, u32[]{:S(2)}, u32[]{:S(2)}) collective-permute-start(f32[1,4,128]{2,1,0:T(4,128)} %get-tuple-element.74), channel_id=1, source_target_pairs={{8,0},{16,8},{24,16},{9,1},{17,9},{25,17},{10,2},{18,10},{26,18},{... | collective-permute-start | bytes 6152 | tf_op jit(solution)/shard_map/ppermute | solution.py:27
  238.8 4.1 %copy-start.12 = (f32[1,4,128]{2,1,0:T(4,128)}, f32[1,4,128]{2,1,0:T(4,128)S(1)}, u32[]{:S(2)}) copy-start(f32[1,4,128]{2,1,0:T(4,128)S(1)} %collective-permute-done.14.refs_5_) | copy-start | bytes 6148
  242.9 0.6 copy-start.15
  242.9 0.6 copy-start.6
  242.9 0.6 copy-start.9

commit v2 on v1

--- a/solution.py
+++ b/solution.py
@@ -31,29 +31,18 @@
     d = jnp.maximum(0.5 * depth_sum, min_depth)
     drive = q - (gravity * step_time / spacing) * d * rise
     power = jnp.exp2(-(7.0 / 3.0) * jnp.log2(d))
-    return drive / (1.0 + (gravity * step_time * 0.5) * rough * jnp.abs(q) * power)
-
-
-def eye_of(tile):
-    return lax.broadcasted_iota(jnp.int32, (tile, tile), 0) == lax.broadcasted_iota(
-        jnp.int32, (tile, tile), 1
-    )
-
-
-def as_row(column, eye):
-    return jnp.sum(jnp.where(eye, column, 0.0), 0, keepdims=True)
-
-
-def as_column(row, eye):
-    return jnp.sum(jnp.where(eye, row, 0.0), 1, keepdims=True)
-
-
-def store_edges(ref, at, slot, x, eye):
+    drag = 1.0 + (gravity * step_time * 0.5) * rough * jnp.abs(q) * power
+    guess = pl.reciprocal(drag, approx=True)
+    return drive * (guess * (2.0 - drag * guess))
+
+
+def store_edges(ref, slot, x):
     tile = x.shape[0]
-    ref[at, pl.ds(slot, 1), :] = x[:1]
-    ref[at + 1, pl.ds(slot, 1), :] = x[tile - 1 :]
-    ref[at + 2, pl.ds(slot, 1), :] = as_row(x[:, :1], eye)
-    ref[at + 3, pl.ds(slot, 1), :] = as_row(x[:, tile - 1 :], eye)
+    turned = x.T
+    ref[0, pl.ds(slot, 1), :] = x[:1]
+    ref[1, pl.ds(slot, 1), :] = x[tile - 1 :]
+    ref[2, pl.ds(slot, 1), :] = turned[:1]
+    ref[3, pl.ds(slot, 1), :] = turned[tile - 1 :]
 
 
 def fill_sends(pick_ref, edge_ref, send_refs, kinds):
@@ -133,12 +122,19 @@
             ref[...] = jnp.zeros_like(ref)
 
     tile = h.shape[1]
-    eye = eye_of(tile)
-    store_edges(edges, 0, slot, ho[0], eye)
-    store_edges(edges, 4, slot, zo[0], eye)
-    store_edges(edges, 8, slot, no[0], eye)
+    lane = lax.broadcasted_iota(jnp.int32, (tile, tile), 1)
+    square = ho[0]
+    for at, x in ((1, zo[0]), (3, no[0]), (5, qo[0, 1])):
+        square = jnp.where(
+            (lane == at) | (lane == at + 1), pltpu.roll(x, at + 1, 1), square
+        )
+    square = square.T
+    for kind, ref in ((0, ho), (4, zo), (8, no)):
+        edges[kind, pl.ds(slot, 1), :] = ref[0, :1, :]
+        edges[kind + 1, pl.ds(slot, 1), :] = ref[0, tile - 1 :, :]
+    for kind, at in ((2, 0), (3, tile - 1), (6, 2), (7, 1), (10, 4), (11, 3), (13, 5)):
+        edges[kind, pl.ds(slot, 1), :] = square[at : at + 1]
     edges[12, pl.ds(slot, 1), :] = qo[0, 0, tile - 1 :, :]
-    edges[13, pl.ds(slot, 1), :] = as_row(qo[0, 1][:, tile - 1 :], eye)
 
     @pl.when(slot == pl.num_programs(0) - 1)
     def _():
@@ -238,48 +234,51 @@
         if first:
             rise_out, rough_out = pop(2)
     halo = pop(1)[0]
-    slot = pl.program_id(0)
+    turn = pl.program_id(0)
     static = (None, rise_out, rough_out) if first else (q_old, rise_in, rough_in)
 
-    @pl.when(slot == 0)
+    @pl.when(turn == 0)
     def _():
         edge_fluxes(first, link, edges, gots, static, halo, flux)
         flux[...] = jnp.where(walls[...] >= 0, flux[...], 0.0)
 
-    h, z, n = h_ref[0], z_ref[0], n_ref[0]
-    tile = h.shape[0]
-    eye = eye_of(tile)
+    group, tile = h_ref.shape[:2]
     row_id = lax.broadcasted_iota(jnp.int32, (tile, tile), 0)
     col_id = lax.broadcasted_iota(jnp.int32, (tile, tile), 1)
-    w = h + z
-
-    def along(dim, q, index, in_edge, out_edge):
-        nxt = functools.partial(pltpu.roll, shift=tile - 1, axis=dim)
-        flow = face(q, h + nxt(h), nxt(w) - w, n + nxt(n))
-        flow = jnp.where(index == tile - 1, out_edge, flow)
-        inflow = jnp.where(index == 0, in_edge, pltpu.roll(flow, 1, dim))
-        return flow, inflow
-
-    def edge(side):
-        return flux[side, pl.ds(slot, 1), :]
-
-    qx, in_x = along(0, q_ref[0, 0], row_id, edge(0), edge(1))
-    qy, in_y = along(
-        1, q_ref[0, 1], col_id, as_column(edge(2), eye), as_column(edge(3), eye)
-    )
-    h = h + (step_time / spacing) * ((in_x - qx) + (in_y - qy))
-    if last:
-        keep = live[slot] >= 0
-        h = jnp.where(keep, h, 0.0)
-        qx = jnp.where(keep, qx, 0.0)
-        qy = jnp.where(keep, qy, 0.0)
-    ho[0] = h
-    qo[0, 0] = qx
-    qo[0, 1] = qy
+
+    for i in range(group):
+        slot = turn * group + i
+        h, z, n = h_ref[i], z_ref[i], n_ref[i]
+        w = h + z
+
+        def along(dim, q, index, in_edge, out_edge):
+            nxt = functools.partial(pltpu.roll, shift=tile - 1, axis=dim)
+            flow = face(q, h + nxt(h), nxt(w) - w, n + nxt(n))
+            flow = jnp.where(index == tile - 1, out_edge, flow)
+            inflow = jnp.where(index == 0, in_edge, pltpu.roll(flow, 1, dim))
+            return flow, inflow
+
+        def edge(side):
+            return flux[side, pl.ds(slot, 1), :]
+
+        columns = jnp.where(row_id == 0, edge(2), jnp.where(row_id == tile - 1, edge(3), 0.0)).T
+        qx, in_x = along(0, q_ref[i, 0], row_id, edge(0), edge(1))
+        qy, in_y = along(1, q_ref[i, 1], col_id, columns, columns)
+        h = h + (step_time / spacing) * ((in_x - qx) + (in_y - qy))
+        if last:
+            keep = live[slot] >= 0
+            h = jnp.where(keep, h, 0.0)
+            qx = jnp.where(keep, qx, 0.0)
+            qy = jnp.where(keep, qy, 0.0)
+        ho[i] = h
+        qo[i, 0] = qx
+        qo[i, 1] = qy
+        if not last:
+            store_edges(edges_out, slot, h)
+
     if not last:
-        store_edges(edges_out, 0, slot, h, eye)
-
-        @pl.when(slot == pl.num_programs(0) - 1)
+
+        @pl.when(turn == pl.num_programs(0) - 1)
         def _():
             fill_sends(pick, edges_out, (s0, s1, s2, s3), LATER_KINDS)
 
@@ -287,8 +286,9 @@
 def step(first, last, link, pick, live, state, edges, gots, static, walls):
     h, q, z, n = state
     slots, tile = h.shape[:2]
-    one = pl.BlockSpec((1, tile, tile), lambda s, *_: (s, 0, 0))
-    two = pl.BlockSpec((1, 2, tile, tile), lambda s, *_: (s, 0, 0, 0))
+    group = 4 if slots % 4 == 0 else 1
+    one = pl.BlockSpec((group, tile, tile), lambda s, *_: (s, 0, 0))
+    two = pl.BlockSpec((group, 2, tile, tile), lambda s, *_: (s, 0, 0, 0))
     table = (4, slots, tile)
     smalls_in = [edges, *gots, *static, walls]
     out_small = []
@@ -301,7 +301,7 @@
         functools.partial(step_kernel, first, last),
         grid_spec=pltpu.PrefetchScalarGridSpec(
             num_scalar_prefetch=3,
-            grid=(slots,),
+            grid=(slots // group,),
             in_specs=[one, two, one, one] + [whole(x.shape) for x in smalls_in],
             out_specs=[one, two] + [whole(s) for s in out_small],
             scratch_shapes=[pltpu.VMEM((4, slots, tile), F32)],
@@ -312,13 +312,60 @@
     )(link, pick, live, h, q, z, n, *smalls_in)
 
 
-def exchange(sends):
-    return [
-        neighbour(sends[1], "gx", -1),
-        neighbour(sends[0], "gx", 1),
-        neighbour(sends[3], "gy", -1),
-        neighbour(sends[2], "gy", 1),
-    ]
+def exchange_kernel(extent, *refs):
+    sends, gots, (sent, landed) = refs[:4], refs[4:8], refs[8:]
+    at = {axis: lax.axis_index(axis) for axis in extent}
+    sides = (("gx", -1), ("gx", 1), ("gy", -1), ("gy", 1))
+    there = [{axis: at[axis] + by} for axis, by in sides]
+    has = [at[axis] > 0 if by < 0 else at[axis] < extent[axis] - 1 for axis, by in sides]
+    barrier = pltpu.get_barrier_semaphore()
+
+    def copy(side):
+        other = OPPOSITE[side]
+        return pltpu.make_async_remote_copy(
+            src_ref=sends[side],
+            dst_ref=gots[other],
+            send_sem=sent.at[side],
+            recv_sem=landed.at[other],
+            device_id=there[side],
+            device_id_type=pl.DeviceIdType.MESH,
+        )
+
+    for side in range(4):
+
+        @pl.when(has[side])
+        def _():
+            pl.semaphore_signal(
+                barrier, inc=1, device_id=there[side], device_id_type=pl.DeviceIdType.MESH
+            )
+
+    pl.semaphore_wait(barrier, sum(x.astype(jnp.int32) for x in has))
+    for side in range(4):
+        pl.when(has[side])(lambda: copy(side).start())
+    for side in range(4):
+
+        @pl.when(has[side])
+        def _():
+            copy(side).wait_send()
+            copy(OPPOSITE[side]).wait_recv()
+
+        @pl.when(jnp.logical_not(has[side]))
+        def _():
+            gots[side][...] = jnp.zeros_like(gots[side])
+
+
+def exchange(turn, sends):
+    extent = {axis: lax.axis_size(axis) for axis in ("gx", "gy")}
+    vmem = pl.BlockSpec(memory_space=pltpu.VMEM)
+    return pl.pallas_call(
+        functools.partial(exchange_kernel, extent),
+        in_specs=[vmem] * 4,
+        out_specs=[vmem] * 4,
+        out_shape=[jax.ShapeDtypeStruct(sends[o].shape, F32) for o in OPPOSITE],
+        scratch_shapes=[pltpu.SemaphoreType.DMA((4,)), pltpu.SemaphoreType.DMA((4,))],
+        compiler_params=pltpu.CompilerParams(collective_id=turn, has_side_effects=True),
+        name="exchange",
+    )(*sends)
 
 
 def shards(depth, discharge, bed, friction, tile_ids, neighbors, moves):
@@ -369,7 +416,7 @@
     static = ()
     for turn in range(STEPS):
         first, last = turn == 0, turn == STEPS - 1
-        gots = exchange(sends)
+        gots = exchange(turn, sends)
         h, q, *rest = step(
             first, last, link, pick, tile_ids, (h, q, z, n), edges, gots, static, walls
         )

time: 271 us -> 178 us (0.66)
  starting transfers between devices: 50.1 us -> 6.45 us
  Pallas kernels: 141 us -> 112 us
  waiting for transfers between devices: 66.1 us -> 49 us
    pallas_call x4, Pallas kernels: 110 us -> 56.8 us  [step(): pl.pallas_call(functools.partial(step_kernel, first, last), grid_spec=plt...]
    ppermute x18 -> x2, starting transfers between devices: 50.1 us -> 6.45 us  [neighbour(): return lax.ppermute(block, axis, route)]
    pallas_call x0 -> x4, Pallas kernels: none -> 25 us  [exchange(): pl.pallas_call(functools.partial(exchange_kernel, extent), in_specs=[vmem...]
    ppermute x18 -> x2, waiting for transfers between devices: 66.1 us -> 49 us  [neighbour(): return lax.ppermute(block, axis, route)]
  transfers between devices with their start and end apart: 18 -> 2, of which waited for: 9 -> 2; matrix products, arithmetic and copies ran while one was open for 2% -> 3% of each run, Pallas kernels for 0% -> 0%
where the time goes in v2:
time: 178 us; the launch traced here: 175 us
  Pallas kernels  112 us (63%)
  waiting for transfers between devices  49 us (28%)
  starting transfers between devices  6.45 us (4%)
  other arithmetic  5.64 us (3%)
    pallas_call x4, Pallas kernels, step(): pl.pallas_call(functools.partial(step_kernel, first, last), grid_spec=plt...  56.8 us
    ppermute x2, waiting for transfers between devices, neighbour(): return lax.ppermute(block, axis, route)  49 us
    pallas_call x4, Pallas kernels, exchange(): pl.pallas_call(functools.partial(exchange_kernel, extent), in_specs=[vmem...  25 us
    pallas_call x1, Pallas kernels, settle(): pl.pallas_call(settle_kernel, grid_spec=pltpu.PrefetchScalarGridSpec(num_...  22.2 us
    pallas_call x1, Pallas kernels, bundle(): pl.pallas_call(bundle_kernel, grid_spec=pltpu.PrefetchScalarGridSpec(num_...  7.83 us
    ppermute x2, starting transfers between devices, neighbour(): return lax.ppermute(block, axis, route)  6.45 us
  transfers between devices with their start and end apart: 2, of which 2 were waited for; matrix products, arithmetic and copies ran while one was open for 3% of the time, Pallas kernels for 0%

profile of v2, /device:TPU:4, one launch (start us, length us, event | category | flops | bytes accessed | tf_op | source)
XLA Modules:
  0.0 175.4 jit_solution(17057092579410835991)
XLA Ops:
  0.6 0.8 compare_select_fusion.1
  1.4 0.6 slice_bitcast_fusion.2
  2.0 0.0 copy-start.1
  2.0 7.8 %bundle.1 = (f32[8,5,128,128]{3,2,1,0:T(8,128)}, f32[8,5,128,128]{3,2,1,0:T(8,128)}) custom-call(s32[8]{0:T(128)} %get-tuple-element.119.down, s32[8]{0:T(128)} %get-tuple-element.118.up, f32[32,128,128]{2,1,0:T(8,128)} %refs_0_.3, f32[32,2,128,128]{3,2,1,0:T(8,128)} %refs_1_.3, f32[32,128,128]{2,1,0:T(8,128)} %refs_2_.3, f32[32,128,128]{2,1,0:T(8,128)} %refs_3_.3, ...), custom_call_target="tpu_custom_call" | custom-call | tf_op jit(solution)/shard_map/bundle/pallas_call | solution.py:84
  9.8 1.9 %collective-permute-start = (f32[8,5,128,128]{3,2,1,0:T(8,128)}, f32[8,5,128,128]{3,2,1,0:T(8,128)S(1)}, u32[]{:S(2)}, u32[]{:S(2)}) collective-permute-start(f32[8,5,128,128]{3,2,1,0:T(8,128)} %get-tuple-element.57), channel_id=1, source_target_pairs={{0,1},{1,2},{2,3},{3,4},{4,5},{5,6},{6,7},{8,9},{9,10},{10,11},{11... | collective-permute-start | bytes 7864328 | tf_op jit(solution)/shard_map/ppermute | solution.py:27
  11.7 4.5 %collective-permute-start.1 = (f32[8,5,128,128]{3,2,1,0:T(8,128)}, f32[8,5,128,128]{3,2,1,0:T(8,128)}, u32[]{:S(2)}, u32[]{:S(2)}) collective-permute-start(f32[8,5,128,128]{3,2,1,0:T(8,128)} %get-tuple-element.58), channel_id=1, source_target_pairs={{1,0},{2,1},{3,2},{4,3},{5,4},{6,5},{7,6},{9,8},{10,9},{11,10},{12... | collective-permute-start | bytes 7864328 | tf_op jit(solution)/shard_map/ppermute | solution.py:27
  16.3 0.1 fusion.4
  16.4 0.6 broadcast_compare_fusion.1
  17.0 0.1 select_reduce_fusion.5
  17.1 0.1 select_reduce_fusion.1
  17.2 0.1 select_reduce_fusion.3
  17.3 0.0 copy-done.1
  17.4 0.3 convert_reduce_fusion
  17.6 0.7 select_reduce_fusion.6.pick
  18.4 0.7 select_reduce_fusion.4.own
  19.1 0.1 select_reduce_fusion.7
  19.2 0.8 select_reduce_fusion.high
  19.9 0.7 select_reduce_fusion.2.low
  20.6 0.6 select_select_fusion.link
  21.2 47.8 %collective-permute-done.refs_4_ = f32[8,5,128,128]{3,2,1,0:T(8,128)S(1)} collective-permute-done((f32[8,5,128,128]{3,2,1,0:T(8,128)}, f32[8,5,128,128]{3,2,1,0:T(8,128)S(1)}, u32[]{:S(2)}, u32[]{:S(2)}) %collective-permute-start) | collective-permute-done | bytes 2621472 | tf_op jit(solution)/shard_map/ppermute | solution.py:27
  69.1 0.0 copy-start
  69.1 1.1 collective-permute-done.1.refs_5_
  70.2 0.4 copy-done
  70.6 22.2 %settle.1 = (f32[32,128,128]{2,1,0:T(8,128)}, f32[32,2,128,128]{3,2,1,0:T(8,128)}, f32[32,128,128]{2,1,0:T(8,128)}, f32[32,128,128]{2,1,0:T(8,128)}, f32[14,32,1...) custom-call(s32[32]{0:T(128)} %get-tuple-element.115.mode, ...), custom_call_target="tpu_custom_call" | custom-call | tf_op jit(solution)/shard_map/settle/pallas_call | solution.py:158
  92.8 7.2 %exchange.4 = (f32[4,4,128]{2,1,0:T(4,128)}, f32[3,4,128]{2,1,0:T(4,128)}, f32[4,8,128]{2,1,0:T(8,128)}, f32[3,8,128]{2,1,0:T(8,128)}) custom-call(f32[3,4,128]{2,1,0:T(4,128)} %get-tuple-element.64.refs_0_, f32[4,4,128]{2,1,0:T(4,128)} %get-tuple-element.65.refs_1_, f32[3,8,128]{2,1,0:T(8,128)} %get-tuple-element.66.refs_2_, ...), custom_call_target="tpu_custom_call" | custom-call | tf_op jit(solution)/shard_map/exchange/pallas_call | solution.py:360
  100.0 0.7 broadcast_in_dim.139.refs_9_.refs_12_
  100.7 16.2 %step.4 = (f32[32,128,128]{2,1,0:T(8,128)}, f32[32,2,128,128]{3,2,1,0:T(8,128)}, f32[4,32,128]{2,1,0:T(8,128)}, f32[1,4,128]{2,1,0:T(4,128)}, f32[1,4,128]{2,1,0...) custom-call(s32[4,32]{1,0:T(4,128)} %select_select_fusion.link, ...), custom_call_target="tpu_custom_call" | custom-call | tf_op jit(solution)/shard_map/step/pallas_call | solution.py:300
  116.9 7.2 %exchange.5 = (f32[1,4,128]{2,1,0:T(4,128)}, f32[1,4,128]{2,1,0:T(4,128)}, f32[1,8,128]{2,1,0:T(8,128)}, f32[1,8,128]{2,1,0:T(8,128)}) custom-call(f32[1,4,128]{2,1,0:T(4,128)} %get-tuple-element.75.refs_0_, f32[1,4,128]{2,1,0:T(4,128)} %get-tuple-element.76.refs_1_, f32[1,8,128]{2,1,0:T(8,128)} %get-tuple-element.77.refs_2_, ...), custom_call_target="tpu_custom_call" | custom-call | tf_op jit(solution)/shard_map/exchange/pallas_call | solution.py:360
  124.1 13.9 %step.5 = (f32[32,128,128]{2,1,0:T(8,128)}, f32[32,2,128,128]{3,2,1,0:T(8,128)}, f32[4,32,128]{2,1,0:T(8,128)}, f32[1,4,128]{2,1,0:T(4,128)}, f32[1,4,128]{2,1,0...) custom-call(s32[4,32]{1,0:T(4,128)} %select_select_fusion.link, ...), custom_call_target="tpu_custom_call" | custom-call | tf_op jit(solution)/shard_map/step/pallas_call | solution.py:300
  138.0 5.4 %exchange.6 = (f32[1,4,128]{2,1,0:T(4,128)}, f32[1,4,128]{2,1,0:T(4,128)}, f32[1,8,128]{2,1,0:T(8,128)}, f32[1,8,128]{2,1,0:T(8,128)}) custom-call(f32[1,4,128]{2,1,0:T(4,128)} %get-tuple-element.89.refs_0_, f32[1,4,128]{2,1,0:T(4,128)} %get-tuple-element.90.refs_1_, f32[1,8,128]{2,1,0:T(8,128)} %get-tuple-element.91.refs_2_, ...), custom_call_target="tpu_custom_call" | custom-call | tf_op jit(solution)/shard_map/exchange/pallas_call | solution.py:360
  143.4 13.9 %step.6 = (f32[32,128,128]{2,1,0:T(8,128)}, f32[32,2,128,128]{3,2,1,0:T(8,128)}, f32[4,32,128]{2,1,0:T(8,128)}, f32[1,4,128]{2,1,0:T(4,128)}, f32[1,4,128]{2,1,0...) custom-call(s32[4,32]{1,0:T(4,128)} %select_select_fusion.link, ...), custom_call_target="tpu_custom_call" | custom-call | tf_op jit(solution)/shard_map/step/pallas_call | solution.py:300
  157.3 5.3 %exchange.7 = (f32[1,4,128]{2,1,0:T(4,128)}, f32[1,4,128]{2,1,0:T(4,128)}, f32[1,8,128]{2,1,0:T(8,128)}, f32[1,8,128]{2,1,0:T(8,128)}) custom-call(f32[1,4,128]{2,1,0:T(4,128)} %get-tuple-element.101.refs_0_, f32[1,4,128]{2,1,0:T(4,128)} %get-tuple-element.102.refs_1_, f32[1,8,128]{2,1,0:T(8,128)} %get-tuple-element.103.refs_2_, ...), custom_call_target="tpu_custom_call" | custom-call | tf_op jit(solution)/shard_map/exchange/pallas_call | solution.py:360
  162.6 12.7 %step.7 = (f32[32,128,128]{2,1,0:T(8,128)}, f32[32,2,128,128]{3,2,1,0:T(8,128)}, f32[4,32,128]{2,1,0:T(8,128)}) custom-call(s32[4,32]{1,0:T(4,128)} %select_select_fusion.link, s32[4,8]{1,0:T(4,128)} %select_reduce_fusion.6.pick, s32[32]{0:T(128)} %live.7, f32[32,128,128]{2,1,0:T(8,128)} %get-tuple-element.98.refs_0_, ...), custom_call_target="tpu_custom_call" | custom-call | tf_op jit(solution)/shard_map/step/pallas_call | solution.py:300
  (5 shorter events, 0.0 us)
Async XLA Ops:
  2.0 15.3 %copy-start.1 = (s32[32,4]{0,1:T(4,128)S(1)}, s32[32,4]{0,1:T(4,128)}, u32[]{:S(2)}) copy-start(s32[32,4]{0,1:T(4,128)} %param.12) | copy-start | bytes 1540
  9.8 59.2 %collective-permute-start = (f32[8,5,128,128]{3,2,1,0:T(8,128)}, f32[8,5,128,128]{3,2,1,0:T(8,128)S(1)}, u32[]{:S(2)}, u32[]{:S(2)}) collective-permute-start(f32[8,5,128,128]{3,2,1,0:T(8,128)} %get-tuple-element.57), channel_id=1, source_target_pairs={{0,1},{1,2},{2,3},{3,4},{4,5},{5,6},{6,7},{8,9},{9,10},{10,11},{11... | collective-permute-start | bytes 7864328 | tf_op jit(solution)/shard_map/ppermute | solution.py:27
  11.7 58.5 %collective-permute-start.1 = (f32[8,5,128,128]{3,2,1,0:T(8,128)}, f32[8,5,128,128]{3,2,1,0:T(8,128)}, u32[]{:S(2)}, u32[]{:S(2)}) collective-permute-start(f32[8,5,128,128]{3,2,1,0:T(8,128)} %get-tuple-element.58), channel_id=1, source_target_pairs={{1,0},{2,1},{3,2},{4,3},{5,4},{6,5},{7,6},{9,8},{10,9},{11,10},{12... | collective-permute-start | bytes 7864328 | tf_op jit(solution)/shard_map/ppermute | solution.py:27
  69.1 1.5 copy-start

commit v3 on v2

--- a/solution.py
+++ b/solution.py
@@ -94,24 +94,36 @@
     )(down, up, depth, discharge, bed, friction, depth, discharge, bed, friction)
 
 
-def settle_kernel(mode, own, low, high, pick, *refs):
-    h, q, z, n, lo, hi, ho, qo, zo, no, edges, s0, s1, s2, s3 = refs
-    slot = pl.program_id(0)
+def settle_kernel(group, mode, own, low, high, pick, *refs):
+    fields, outs = refs[: 6 * group], refs[6 * group :]
+    edges, sends = outs[4], outs[5:]
+    turn = pl.program_id(0)
+    for i in range(group):
+        settle_one(i, turn * group + i, mode, *fields[6 * i : 6 * i + 6], *outs[:4])
+    for i in range(group):
+        settled_edges(i, turn * group + i, *outs[:5])
+
+    @pl.when(turn == pl.num_programs(0) - 1)
+    def _():
+        fill_sends(pick, edges, sends, FIRST_KINDS)
+
+
+def settle_one(i, slot, mode, h, q, z, n, lo, hi, ho, qo, zo, no):
     kind = mode[slot]
 
     @pl.when(kind == 0)
     def _():
-        ho[...] = h[...]
-        qo[...] = q[...]
-        zo[...] = z[...]
-        no[...] = n[...]
+        ho[i] = h[0]
+        qo[i] = q[0]
+        zo[i] = z[0]
+        no[i] = n[0]
 
     def take(src):
-        ho[0] = src[0, 0]
-        qo[0, 0] = src[0, 1]
-        qo[0, 1] = src[0, 2]
-        zo[0] = src[0, 3]
-        no[0] = src[0, 4]
+        ho[i] = src[0, 0]
+        qo[i, 0] = src[0, 1]
+        qo[i, 1] = src[0, 2]
+        zo[i] = src[0, 3]
+        no[i] = src[0, 4]
 
     pl.when(kind == 1)(lambda: take(lo))
     pl.when(kind == 2)(lambda: take(hi))
@@ -119,56 +131,66 @@
     @pl.when(kind == 3)
     def _():
         for ref in (ho, qo, zo, no):
-            ref[...] = jnp.zeros_like(ref)
-
-    tile = h.shape[1]
+            ref[i] = jnp.zeros(ref.shape[1:], F32)
+
+
+def settled_edges(i, slot, ho, qo, zo, no, edges):
+    tile = ho.shape[1]
     lane = lax.broadcasted_iota(jnp.int32, (tile, tile), 1)
-    square = ho[0]
-    for at, x in ((1, zo[0]), (3, no[0]), (5, qo[0, 1])):
+    square = ho[i]
+    for at, x in ((1, zo[i]), (3, no[i]), (5, qo[i, 1])):
         square = jnp.where(
             (lane == at) | (lane == at + 1), pltpu.roll(x, at + 1, 1), square
         )
     square = square.T
     for kind, ref in ((0, ho), (4, zo), (8, no)):
-        edges[kind, pl.ds(slot, 1), :] = ref[0, :1, :]
-        edges[kind + 1, pl.ds(slot, 1), :] = ref[0, tile - 1 :, :]
+        edges[kind, pl.ds(slot, 1), :] = ref[i, :1, :]
+        edges[kind + 1, pl.ds(slot, 1), :] = ref[i, tile - 1 :, :]
     for kind, at in ((2, 0), (3, tile - 1), (6, 2), (7, 1), (10, 4), (11, 3), (13, 5)):
         edges[kind, pl.ds(slot, 1), :] = square[at : at + 1]
-    edges[12, pl.ds(slot, 1), :] = qo[0, 0, tile - 1 :, :]
-
-    @pl.when(slot == pl.num_programs(0) - 1)
-    def _():
-        fill_sends(pick, edges, (s0, s1, s2, s3), FIRST_KINDS)
+    edges[12, pl.ds(slot, 1), :] = qo[i, 0, tile - 1 :, :]
 
 
 def whole(shape):
     return pl.BlockSpec(shape, lambda *_: (0,) * len(shape))
 
 
-def settle(mode, own, low, high, pick, depth, discharge, bed, friction, got_low, got_high):
+def group_of(slots, most):
+    return most if slots % most == 0 else 1
+
+
+def settle(group, mode, own, low, high, pick, depth, discharge, bed, friction, got_low, got_high):
     slots, tile = depth.shape[:2]
-    one = pl.BlockSpec((1, tile, tile), lambda s, m, o, l, h, p: (o[s], 0, 0))
-    two = pl.BlockSpec((1, 2, tile, tile), lambda s, m, o, l, h, p: (o[s], 0, 0, 0))
-    lo = pl.BlockSpec((1, 5, tile, tile), lambda s, m, o, l, h, p: (l[s], 0, 0, 0))
-    hi = pl.BlockSpec((1, 5, tile, tile), lambda s, m, o, l, h, p: (h[s], 0, 0, 0))
-    out1 = pl.BlockSpec((1, tile, tile), lambda s, *_: (s, 0, 0))
-    out2 = pl.BlockSpec((1, 2, tile, tile), lambda s, *_: (s, 0, 0, 0))
+
+    def block(i, lead, table):
+        rest = (0,) * (len(lead) + 2)
+        return pl.BlockSpec(
+            (1, *lead, tile, tile), lambda s, *tables: (tables[table][s * group + i], *rest)
+        )
+
+    ins = []
+    for i in range(group):
+        one, two = block(i, (), 1), block(i, (2,), 1)
+        ins += [one, two, one, one, block(i, (5,), 2), block(i, (5,), 3)]
+    out1 = pl.BlockSpec((group, tile, tile), lambda s, *_: (s, 0, 0))
+    out2 = pl.BlockSpec((group, 2, tile, tile), lambda s, *_: (s, 0, 0, 0))
     sends = [(len(k), c, tile) for k, c in zip(FIRST_KINDS, COUNTS)]
     small = [(14, slots, tile)] + sends
     return pl.pallas_call(
-        settle_kernel,
+        functools.partial(settle_kernel, group),
         grid_spec=pltpu.PrefetchScalarGridSpec(
             num_scalar_prefetch=5,
-            grid=(slots,),
-            in_specs=[one, two, one, one, lo, hi],
+            grid=(slots // group,),
+            in_specs=ins,
             out_specs=[out1, out2, out1, out1] + [whole(s) for s in small],
         ),
         out_shape=[
             jax.ShapeDtypeStruct(x.shape, F32) for x in (depth, discharge, bed, friction)
         ]
         + [jax.ShapeDtypeStruct(s, F32) for s in small],
+        compiler_params=pltpu.CompilerParams(vmem_limit_bytes=32 * 2**20),
         name="settle",
-    )(mode, own, low, high, pick, depth, discharge, bed, friction, got_low, got_high)
+    )(mode, own, low, high, pick, *[depth, discharge, bed, friction, got_low, got_high] * group)
 
 
 def edge_fluxes(first, link, edges, gots, static, halo, flux):
@@ -286,7 +308,7 @@
 def step(first, last, link, pick, live, state, edges, gots, static, walls):
     h, q, z, n = state
     slots, tile = h.shape[:2]
-    group = 4 if slots % 4 == 0 else 1
+    group = group_of(slots, 8)
     one = pl.BlockSpec((group, tile, tile), lambda s, *_: (s, 0, 0))
     two = pl.BlockSpec((group, 2, tile, tile), lambda s, *_: (s, 0, 0, 0))
     table = (4, slots, tile)
@@ -308,6 +330,7 @@
         ),
         out_shape=[jax.ShapeDtypeStruct(h.shape, F32), jax.ShapeDtypeStruct(q.shape, F32)]
         + [jax.ShapeDtypeStruct(s, F32) for s in out_small],
+        compiler_params=pltpu.CompilerParams(vmem_limit_bytes=32 * 2**20),
         name="step",
     )(link, pick, live, h, q, z, n, *smalls_in)
 
@@ -374,6 +397,9 @@
     base = owner_id * slots
     plan = moves[0]
     slot_id = jnp.arange(slots)
+    group = group_of(slots, 4)
+    together = slot_id[None] % group == slot_id[:, None] % group
+    earlier = together & (slot_id[None] <= slot_id[:, None])
 
     leave = jnp.where(plan[:, :, 0] >= 0, plan[:, :, 0] - base, slots)
     land = jnp.where(plan[:, :, 1] >= 0, plan[:, :, 1] - base, slots)
@@ -391,7 +417,7 @@
 
     def carried(used, value):
         seen = jnp.max(
-            jnp.where(used[None] & (slot_id[None] <= slot_id[:, None]), slot_id[None], -1), 1
+            jnp.where(used[None] & earlier, slot_id[None], -1), 1
         )
         return jnp.sum(jnp.where(seen[:, None] == slot_id[None], value[None], 0), 1)
 
@@ -411,7 +437,7 @@
     mode, own, low, high, link, pick = as_int(mode, own, low, high, link, pick)
 
     h, q, z, n, edges, *sends = settle(
-        mode, own, low, high, pick, depth, discharge, bed, friction, from_low, from_high
+        group, mode, own, low, high, pick, depth, discharge, bed, friction, from_low, from_high
     )
     static = ()
     for turn in range(STEPS):

time: 178 us -> 203 us (1.14)
  local copies, waits for them, and re-layouts: 1.73 us -> 61.9 us
  Pallas kernels: 112 us -> 78 us
  other arithmetic: 5.64 us -> 2.16 us
  waiting for transfers between devices: 49 us -> 52 us
    unnamed x4 -> x122, local copies, waits for them, and re-layouts: 0.4 us -> 61.3 us
    pallas_call x4, Pallas kernels: 56.8 us -> 37.7 us  [step(): pl.pallas_call(functools.partial(step_kernel, first, last), grid_spec=plt...]
    pallas_call x1, Pallas kernels: 22.2 us -> 7.89 us  [settle(): pl.pallas_call(functools.partial(settle_kernel, group), grid_spec=pltpu.P...]
    ppermute x2, waiting for transfers between devices: 49 us -> 52 us  [neighbour(): return lax.ppermute(block, axis, route)]
  transfers between devices with their start and end apart: 2 -> 2, of which waited for: 2 -> 2; matrix products, arithmetic and copies ran while one was open for 3% -> 1% of each run, Pallas kernels for 0% -> 0%
where the time goes in v3:
time: 203 us; the launch traced here: 201 us
  Pallas kernels  78 us (38%)
  local copies, waits for them, and re-layouts  61.9 us (30%)
  waiting for transfers between devices  52 us (26%)
  starting transfers between devices  6.45 us (3%)
  other arithmetic  2.16 us (1%)
    unnamed x122, local copies, waits for them, and re-layouts  61.3 us
    ppermute x2, waiting for transfers between devices, neighbour(): return lax.ppermute(block, axis, route)  52 us
    pallas_call x4, Pallas kernels, step(): pl.pallas_call(functools.partial(step_kernel, first, last), grid_spec=plt...  37.7 us
    pallas_call x4, Pallas kernels, exchange(): pl.pallas_call(functools.partial(exchange_kernel, extent), in_specs=[vmem...  24.6 us
    pallas_call x1, Pallas kernels, settle(): pl.pallas_call(functools.partial(settle_kernel, group), grid_spec=pltpu.P...  7.89 us
    pallas_call x1, Pallas kernels, bundle(): pl.pallas_call(bundle_kernel, grid_spec=pltpu.PrefetchScalarGridSpec(num_...  7.86 us
    ppermute x2, starting transfers between devices, neighbour(): return lax.ppermute(block, axis, route)  6.45 us
  transfers between devices with their start and end apart: 2, of which 2 were waited for; matrix products, arithmetic and copies ran while one was open for 1% of the time, Pallas kernels for 0%

profile of v3, /device:TPU:4, one launch (start us, length us, event | category | flops | bytes accessed | tf_op | source)
XLA Modules:
  0.0 201.5 jit_solution(13107187150704521472)
XLA Ops:
  0.6 0.8 compare_select_fusion.1
  1.9 7.9 %bundle.1 = (f32[8,5,128,128]{3,2,1,0:T(8,128)}, f32[8,5,128,128]{3,2,1,0:T(8,128)}) custom-call(s32[8]{0:T(128)} %get-tuple-element.122.down, s32[8]{0:T(128)} %get-tuple-element.121.up, f32[32,128,128]{2,1,0:T(8,128)} %refs_18_.1, f32[32,2,128,128]{3,2,1,0:T(8,128)} %refs_19_.1, f32[32,128,128]{2,1,0:T(8,128)} %refs_20_.1, f32[32,128,128]{2,1,0:T(8,128)} %refs_21_.1, ...), custom_call_target="tpu_custom_call" | custom-call | tf_op jit(solution)/shard_map/bundle/pallas_call | solution.py:84
  9.8 1.9 collective-permute-start
  11.7 4.5 %collective-permute-start.1 = (f32[8,5,128,128]{3,2,1,0:T(8,128)}, f32[8,5,128,128]{3,2,1,0:T(8,128)S(1)}, u32[]{:S(2)}, u32[]{:S(2)}) collective-permute-start(f32[8,5,128,128]{3,2,1,0:T(8,128)} %get-tuple-element.58), channel_id=1, source_target_pairs={{1,0},{2,1},{3,2},{4,3},{5,4},{6,5},{7,6},{9,8},{10,9},{11,10},{12... | collective-permute-start | bytes 7864328 | tf_op jit(solution)/shard_map/ppermute | solution.py:27
  17.7 51.4 %collective-permute-done.refs_4_.refs_10_.refs_16_.refs_22_ = f32[8,5,128,128]{3,2,1,0:T(8,128)S(1)} collective-permute-done((f32[8,5,128,128]{3,2,1,0:T(8,128)}, f32[8,5,128,128]{3,2,1,0:T(8,128)S(1)}, u32[]{:S(2)}, u32[]{:S(2)}) %collective-permute-start) | collective-permute-done | bytes 2621472 | tf_op jit(solution)/shard_map/ppermute | solution.py:27
  69.2 0.6 collective-permute-done.1.refs_5_.refs_11_.refs_17_.refs_23_
  69.8 1.6 copy-done.1
  71.4 1.6 copy-done.2
  73.0 7.9 %settle.1 = (f32[32,128,128]{2,1,0:T(8,128)S(1)}, f32[32,2,128,128]{3,2,1,0:T(8,128)S(1)}, f32[32,128,128]{2,1,0:T(8,128)S(1)}, f32[32,128,128]{2,1,0:T(8,128)S(...) custom-call(s32[32]{0:T(128)S(1)} %get-tuple-element.118.mode, ...), custom_call_target="tpu_custom_call" | custom-call | tf_op jit(solution)/shard_map/settle/pallas_call | solution.py:179
  80.9 1.3 copy-done.3
  82.2 1.3 copy-done.6
  83.5 2.0 copy-done.11
  85.6 1.3 copy-done.19
  86.9 0.6 copy-done.28
  87.5 0.6 copy-done.30
  88.1 0.6 copy-done.33
  88.7 0.6 copy-done.35
  89.3 7.8 %exchange.4 = (f32[4,4,128]{2,1,0:T(4,128)}, f32[3,4,128]{2,1,0:T(4,128)}, f32[4,8,128]{2,1,0:T(8,128)}, f32[3,8,128]{2,1,0:T(8,128)}) custom-call(f32[3,4,128]{2,1,0:T(4,128)} %copy-done.35, f32[4,4,128]{2,1,0:T(4,128)} %copy-done.33, f32[3,8,128]{2,1,0:T(8,128)} %copy-done.30, f32[4,8,128]{2,1,0:T(8,128)} %copy-done.28), custom_call_target="tpu_custom_call" | custom-call | tf_op jit(solution)/shard_map/exchange/pallas_call | solution.py:383
  97.1 1.6 copy-done.4
  98.7 1.6 copy-done.7
  100.3 2.2 %copy-done.12 = f32[32,2,128,128]{3,2,1,0:T(8,128)S(1)} copy-done((f32[32,2,128,128]{3,2,1,0:T(8,128)S(1)}, f32[32,2,128,128]{3,2,1,0:T(8,128)}, u32[]{:S(2)}) %copy-start.12) | copy-done | bytes 4194328
  102.5 1.6 copy-done.20
  104.1 0.7 copy-done.27
  104.8 0.7 copy-done.29
  105.5 0.7 copy-done.31
  106.2 0.7 copy-done.34
  106.9 11.1 %step.4 = (f32[32,128,128]{2,1,0:T(8,128)S(1)}, f32[32,2,128,128]{3,2,1,0:T(8,128)S(1)}, f32[4,32,128]{2,1,0:T(8,128)S(1)}, f32[1,4,128]{2,1,0:T(4,128)S(1)}, f3...) custom-call(s32[4,32]{1,0:T(4,128)S(1)} %select_select_fusion.link, ...), custom_call_target="tpu_custom_call" | custom-call | tf_op jit(solution)/shard_map/step/pallas_call | solution.py:322
  118.0 2.0 copy-done.15
  120.0 1.3 copy-done.23
  121.3 0.6 copy-done.42
  121.9 0.6 copy-done.43
  122.5 0.6 copy-done.48
  123.7 6.1 %exchange.5 = (f32[1,4,128]{2,1,0:T(4,128)}, f32[1,4,128]{2,1,0:T(4,128)}, f32[1,8,128]{2,1,0:T(8,128)}, f32[1,8,128]{2,1,0:T(8,128)}) custom-call(f32[1,4,128]{2,1,0:T(4,128)} %copy-done.48, f32[1,4,128]{2,1,0:T(4,128)} %copy-done.49, f32[1,8,128]{2,1,0:T(8,128)} %copy-done.42, f32[1,8,128]{2,1,0:T(8,128)} %copy-done.43), custom_call_target="tpu_custom_call" | custom-call | tf_op jit(solution)/shard_map/exchange/pallas_call | solution.py:383
  129.8 1.6 copy-done.8
  131.4 2.2 %copy-done.16 = f32[32,2,128,128]{3,2,1,0:T(8,128)S(1)} copy-done((f32[32,2,128,128]{3,2,1,0:T(8,128)S(1)}, f32[32,2,128,128]{3,2,1,0:T(8,128)}, u32[]{:S(2)}) %copy-start.16) | copy-done | bytes 4194328
  133.6 1.6 copy-done.24
  135.2 0.7 copy-done.38
  135.9 0.7 copy-done.39
  136.5 0.7 copy-done.56
  137.2 0.7 copy-done.57
  137.9 8.9 %step.5 = (f32[32,128,128]{2,1,0:T(8,128)S(1)}, f32[32,2,128,128]{3,2,1,0:T(8,128)S(1)}, f32[4,32,128]{2,1,0:T(8,128)S(1)}, f32[1,4,128]{2,1,0:T(4,128)S(1)}, f3...) custom-call(s32[4,32]{1,0:T(4,128)S(1)} %select_select_fusion.link, ...), custom_call_target="tpu_custom_call" | custom-call | tf_op jit(solution)/shard_map/step/pallas_call | solution.py:322
  146.8 2.0 copy-done.17
  148.9 1.3 copy-done.25
  151.3 0.6 copy-done.45
  151.9 5.3 %exchange.6 = (f32[1,4,128]{2,1,0:T(4,128)}, f32[1,4,128]{2,1,0:T(4,128)}, f32[1,8,128]{2,1,0:T(8,128)}, f32[1,8,128]{2,1,0:T(8,128)}) custom-call(f32[1,4,128]{2,1,0:T(4,128)} %copy-done.50, f32[1,4,128]{2,1,0:T(4,128)} %copy-done.51, f32[1,8,128]{2,1,0:T(8,128)} %copy-done.44, f32[1,8,128]{2,1,0:T(8,128)} %copy-done.45), custom_call_target="tpu_custom_call" | custom-call | tf_op jit(solution)/shard_map/exchange/pallas_call | solution.py:383
  157.3 1.6 copy-done.9
  158.9 2.2 %copy-done.18 = f32[32,2,128,128]{3,2,1,0:T(8,128)S(1)} copy-done((f32[32,2,128,128]{3,2,1,0:T(8,128)S(1)}, f32[32,2,128,128]{3,2,1,0:T(8,128)}, u32[]{:S(2)}) %copy-start.18) | copy-done | bytes 4194328
  161.1 1.6 copy-done.26
  162.7 0.7 copy-done.40
  163.3 0.7 copy-done.41
  164.0 0.6 copy-done.58
  164.7 0.7 copy-done.59
  165.3 8.9 %step.6 = (f32[32,128,128]{2,1,0:T(8,128)S(1)}, f32[32,2,128,128]{3,2,1,0:T(8,128)S(1)}, f32[4,32,128]{2,1,0:T(8,128)S(1)}, f32[1,4,128]{2,1,0:T(4,128)S(1)}, f3...) custom-call(s32[4,32]{1,0:T(4,128)S(1)} %select_select_fusion.link, ...), custom_call_target="tpu_custom_call" | custom-call | tf_op jit(solution)/shard_map/step/pallas_call | solution.py:322
  174.2 2.0 copy-done.13
  176.3 1.3 copy-done.21
  179.3 5.3 %exchange.7 = (f32[1,4,128]{2,1,0:T(4,128)}, f32[1,4,128]{2,1,0:T(4,128)}, f32[1,8,128]{2,1,0:T(8,128)}, f32[1,8,128]{2,1,0:T(8,128)}) custom-call(f32[1,4,128]{2,1,0:T(4,128)} %copy-done.52, f32[1,4,128]{2,1,0:T(4,128)} %copy-done.53, f32[1,8,128]{2,1,0:T(8,128)} %copy-done.46, f32[1,8,128]{2,1,0:T(8,128)} %copy-done.47), custom_call_target="tpu_custom_call" | custom-call | tf_op jit(solution)/shard_map/exchange/pallas_call | solution.py:383
  184.6 1.6 copy-done.10
  186.2 2.2 %copy-done.14 = f32[32,2,128,128]{3,2,1,0:T(8,128)S(1)} copy-done((f32[32,2,128,128]{3,2,1,0:T(8,128)S(1)}, f32[32,2,128,128]{3,2,1,0:T(8,128)}, u32[]{:S(2)}) %copy-start.14) | copy-done | bytes 4194328
  188.4 1.6 copy-done.22
  190.0 0.7 copy-done.36
  190.7 0.7 copy-done.37
  191.4 0.7 copy-done.54
  192.0 0.7 copy-done.55
  192.7 8.8 %step.7 = (f32[32,128,128]{2,1,0:T(8,128)}, f32[32,2,128,128]{3,2,1,0:T(8,128)}, f32[4,32,128]{2,1,0:T(8,128)}) custom-call(s32[4,32]{1,0:T(4,128)S(1)} %select_select_fusion.link, s32[4,8]{1,0:T(4,128)S(1)} %select_reduce_fusion.6.pick, s32[32]{0:T(128)S(1)} %copy-done.32, f32[32,128,128]{2,1,0:T(8,128)S(1)} %copy-done.22, ...), custom_call_target="tpu_custom_call" | custom-call | tf_op jit(solution)/shard_map/step/pallas_call | solution.py:322
  (91 shorter events, 5.6 us)
Async XLA Ops:
  1.9 14.4 %copy-start.60 = (s32[32,4]{0,1:T(4,128)S(1)}, s32[32,4]{0,1:T(4,128)}, u32[]{:S(2)}) copy-start(s32[32,4]{0,1:T(4,128)} %param.12) | copy-start | bytes 1540
  1.9 67.8 %copy-start = (f32[32,128,128]{2,1,0:T(8,128)S(1)}, f32[32,128,128]{2,1,0:T(8,128)}, u32[]{:S(2)}) copy-start(f32[32,128,128]{2,1,0:T(8,128)} %refs_18_.1) | copy-start | bytes 6291460
  9.8 59.4 %collective-permute-start = (f32[8,5,128,128]{3,2,1,0:T(8,128)}, f32[8,5,128,128]{3,2,1,0:T(8,128)S(1)}, u32[]{:S(2)}, u32[]{:S(2)}) collective-permute-start(f32[8,5,128,128]{3,2,1,0:T(8,128)} %get-tuple-element.57), channel_id=1, source_target_pairs={{0,1},{1,2},{2,3},{3,4},{4,5},{5,6},{6,7},{8,9},{9,10},{10,11},{11... | collective-permute-start | bytes 7864328 | tf_op jit(solution)/shard_map/ppermute | solution.py:27
  11.7 58.1 %collective-permute-start.1 = (f32[8,5,128,128]{3,2,1,0:T(8,128)}, f32[8,5,128,128]{3,2,1,0:T(8,128)S(1)}, u32[]{:S(2)}, u32[]{:S(2)}) collective-permute-start(f32[8,5,128,128]{3,2,1,0:T(8,128)} %get-tuple-element.58), channel_id=1, source_target_pairs={{1,0},{2,1},{3,2},{4,3},{5,4},{6,5},{7,6},{9,8},{10,9},{11,10},{12... | collective-permute-start | bytes 7864328 | tf_op jit(solution)/shard_map/ppermute | solution.py:27
  69.8 1.6 copy-start.1
  71.4 1.6 copy-start.2
  73.0 24.2 %copy-start.32 = (s32[32]{0:T(128)S(1)}, s32[32]{0:T(128)}, u32[]{:S(2)}) copy-start(s32[32]{0:T(128)} %live.7) | copy-start | bytes 388
  80.9 1.3 copy-start.3
  82.2 1.4 copy-start.6
  83.5 2.0 copy-start.11
  85.6 1.3 copy-start.19
  86.9 0.6 copy-start.28
  87.5 0.6 copy-start.30
  88.1 0.6 copy-start.33
  88.7 0.6 copy-start.35
  97.1 1.6 copy-start.4
  98.7 1.6 copy-start.7
  100.3 2.2 %copy-start.12 = (f32[32,2,128,128]{3,2,1,0:T(8,128)S(1)}, f32[32,2,128,128]{3,2,1,0:T(8,128)}, u32[]{:S(2)}) copy-start(f32[32,2,128,128]{3,2,1,0:T(8,128)} %copy-done.11) | copy-start | bytes 12582916
  102.5 1.6 copy-start.20
  104.1 0.7 copy-start.27
  104.8 0.7 copy-start.29
  105.5 0.7 copy-start.31
  106.2 0.7 copy-start.34
  106.9 22.9 %copy-start.5 = (f32[32,128,128]{2,1,0:T(8,128)S(1)}, f32[32,128,128]{2,1,0:T(8,128)}, u32[]{:S(2)}) copy-start(f32[32,128,128]{2,1,0:T(8,128)} %copy-done.3) | copy-start | bytes 6291460
  118.0 2.0 %copy-start.15 = (f32[32,2,128,128]{3,2,1,0:T(8,128)}, f32[32,2,128,128]{3,2,1,0:T(8,128)S(1)}, u32[]{:S(2)}) copy-start(f32[32,2,128,128]{3,2,1,0:T(8,128)S(1)} %get-tuple-element.73.refs_1_) | copy-start | bytes 12582916
  120.0 1.3 copy-start.23
  121.3 0.6 copy-start.42
  121.9 0.6 copy-start.43
  122.5 0.6 copy-start.48
  123.1 0.6 copy-start.49
  129.8 1.6 copy-start.8
  131.4 2.2 %copy-start.16 = (f32[32,2,128,128]{3,2,1,0:T(8,128)S(1)}, f32[32,2,128,128]{3,2,1,0:T(8,128)}, u32[]{:S(2)}) copy-start(f32[32,2,128,128]{3,2,1,0:T(8,128)} %copy-done.15) | copy-start | bytes 12582916
  133.6 1.6 copy-start.24
  135.2 0.7 copy-start.38
  135.9 0.7 copy-start.39
  136.5 0.7 copy-start.56
  137.2 0.7 copy-start.57
  146.8 2.0 %copy-start.17 = (f32[32,2,128,128]{3,2,1,0:T(8,128)}, f32[32,2,128,128]{3,2,1,0:T(8,128)S(1)}, u32[]{:S(2)}) copy-start(f32[32,2,128,128]{3,2,1,0:T(8,128)S(1)} %get-tuple-element.87.refs_1_) | copy-start | bytes 12582916
  148.9 1.3 copy-start.25
  150.2 0.6 copy-start.44
  150.8 0.6 copy-start.51
  151.3 0.6 copy-start.45
  151.3 0.6 copy-start.50
  157.3 1.6 copy-start.9
  158.9 2.2 %copy-start.18 = (f32[32,2,128,128]{3,2,1,0:T(8,128)S(1)}, f32[32,2,128,128]{3,2,1,0:T(8,128)}, u32[]{:S(2)}) copy-start(f32[32,2,128,128]{3,2,1,0:T(8,128)} %copy-done.17) | copy-start | bytes 12582916
  161.1 1.6 copy-start.26
  162.7 0.7 copy-start.40
  163.3 0.7 copy-start.41
  164.0 0.6 copy-start.58
  164.6 0.7 copy-start.59
  174.2 2.0 %copy-start.13 = (f32[32,2,128,128]{3,2,1,0:T(8,128)}, f32[32,2,128,128]{3,2,1,0:T(8,128)S(1)}, u32[]{:S(2)}) copy-start(f32[32,2,128,128]{3,2,1,0:T(8,128)S(1)} %get-tuple-element.99.refs_1_) | copy-start | bytes 12582916
  176.3 1.3 copy-start.21
  177.6 0.6 copy-start.46
  178.2 0.6 copy-start.53
  178.7 0.6 copy-start.47
  178.7 0.6 copy-start.52
  184.6 1.6 copy-start.10
  186.2 2.2 %copy-start.14 = (f32[32,2,128,128]{3,2,1,0:T(8,128)S(1)}, f32[32,2,128,128]{3,2,1,0:T(8,128)}, u32[]{:S(2)}) copy-start(f32[32,2,128,128]{3,2,1,0:T(8,128)} %copy-done.13) | copy-start | bytes 12582916
  188.4 1.6 copy-start.22
  190.0 0.7 copy-start.36
  190.7 0.7 copy-start.37
  191.4 0.7 copy-start.54
  192.0 0.7 copy-start.55

commit v4 on v3

--- a/solution.py
+++ b/solution.py
@@ -188,7 +188,6 @@
             jax.ShapeDtypeStruct(x.shape, F32) for x in (depth, discharge, bed, friction)
         ]
         + [jax.ShapeDtypeStruct(s, F32) for s in small],
-        compiler_params=pltpu.CompilerParams(vmem_limit_bytes=32 * 2**20),
         name="settle",
     )(mode, own, low, high, pick, *[depth, discharge, bed, friction, got_low, got_high] * group)
 
@@ -330,7 +329,6 @@
         ),
         out_shape=[jax.ShapeDtypeStruct(h.shape, F32), jax.ShapeDtypeStruct(q.shape, F32)]
         + [jax.ShapeDtypeStruct(s, F32) for s in out_small],
-        compiler_params=pltpu.CompilerParams(vmem_limit_bytes=32 * 2**20),
         name="step",
     )(link, pick, live, h, q, z, n, *smalls_in)
 

time: 203 us -> 162 us (0.80)
  local copies, waits for them, and re-layouts: 61.9 us -> 1.34 us
  Pallas kernels: 78 us -> 97.5 us
  other arithmetic: 2.16 us -> 5.52 us
  waiting for transfers between devices: 52 us -> 49.5 us
    unnamed x122 -> x4, local copies, waits for them, and re-layouts: 61.3 us -> 0.01 us
    pallas_call x4, Pallas kernels: 37.7 us -> 52.4 us  [step(): pl.pallas_call(functools.partial(step_kernel, first, last), grid_spec=plt...]
    pallas_call x1, Pallas kernels: 7.89 us -> 13.4 us  [settle(): pl.pallas_call(functools.partial(settle_kernel, group), grid_spec=pltpu.P...]
    ppermute x2, waiting for transfers between devices: 52 us -> 49.5 us  [neighbour(): return lax.ppermute(block, axis, route)]
  transfers between devices with their start and end apart: 2 -> 2, of which waited for: 2 -> 2; matrix products, arithmetic and copies ran while one was open for 1% -> 3% of each run, Pallas kernels for 0% -> 0%
where the time goes in v4:
time: 162 us; the launch traced here: 161 us
  Pallas kernels  97.5 us (60%)
  waiting for transfers between devices  49.5 us (31%)
  starting transfers between devices  6.45 us (4%)
  other arithmetic  5.52 us (3%)
    pallas_call x4, Pallas kernels, step(): pl.pallas_call(functools.partial(step_kernel, first, last), grid_spec=plt...  52.4 us
    ppermute x2, waiting for transfers between devices, neighbour(): return lax.ppermute(block, axis, route)  49.5 us
    pallas_call x4, Pallas kernels, exchange(): pl.pallas_call(functools.partial(exchange_kernel, extent), in_specs=[vmem...  24.2 us
    pallas_call x1, Pallas kernels, settle(): pl.pallas_call(functools.partial(settle_kernel, group), grid_spec=pltpu.P...  13.4 us
    pallas_call x1, Pallas kernels, bundle(): pl.pallas_call(bundle_kernel, grid_spec=pltpu.PrefetchScalarGridSpec(num_...  7.47 us
    ppermute x2, starting transfers between devices, neighbour(): return lax.ppermute(block, axis, route)  6.45 us
  transfers between devices with their start and end apart: 2, of which 2 were waited for; matrix products, arithmetic and copies ran while one was open for 3% of the time, Pallas kernels for 0%

profile of v4, /device:TPU:4, one launch (start us, length us, event | category | flops | bytes accessed | tf_op | source)
XLA Modules:
  0.0 161.0 jit_solution(7156628195073258371)
XLA Ops:
  0.6 0.8 compare_select_fusion.1
  1.4 0.6 slice_bitcast_fusion.2
  2.0 0.0 copy-start.1
  2.0 7.5 %bundle.1 = (f32[8,5,128,128]{3,2,1,0:T(8,128)}, f32[8,5,128,128]{3,2,1,0:T(8,128)}) custom-call(s32[8]{0:T(128)} %get-tuple-element.122.down, s32[8]{0:T(128)} %get-tuple-element.121.up, f32[32,128,128]{2,1,0:T(8,128)} %refs_18_.1, f32[32,2,128,128]{3,2,1,0:T(8,128)} %refs_19_.1, f32[32,128,128]{2,1,0:T(8,128)} %refs_20_.1, f32[32,128,128]{2,1,0:T(8,128)} %refs_21_.1, ...), custom_call_target="tpu_custom_call" | custom-call | tf_op jit(solution)/shard_map/bundle/pallas_call | solution.py:84
  9.5 2.1 %collective-permute-start = (f32[8,5,128,128]{3,2,1,0:T(8,128)}, f32[8,5,128,128]{3,2,1,0:T(8,128)S(1)}, u32[]{:S(2)}, u32[]{:S(2)}) collective-permute-start(f32[8,5,128,128]{3,2,1,0:T(8,128)} %get-tuple-element.57), channel_id=1, source_target_pairs={{0,1},{1,2},{2,3},{3,4},{4,5},{5,6},{6,7},{8,9},{9,10},{10,11},{11... | collective-permute-start | bytes 7864328 | tf_op jit(solution)/shard_map/ppermute | solution.py:27
  11.6 4.4 %collective-permute-start.1 = (f32[8,5,128,128]{3,2,1,0:T(8,128)}, f32[8,5,128,128]{3,2,1,0:T(8,128)}, u32[]{:S(2)}, u32[]{:S(2)}) collective-permute-start(f32[8,5,128,128]{3,2,1,0:T(8,128)} %get-tuple-element.58), channel_id=1, source_target_pairs={{1,0},{2,1},{3,2},{4,3},{5,4},{6,5},{7,6},{9,8},{10,9},{11,10},{12... | collective-permute-start | bytes 7864328 | tf_op jit(solution)/shard_map/ppermute | solution.py:27
  16.0 0.0 copy-done.1
  16.0 0.3 convert_reduce_fusion
  16.3 0.7 select_reduce_fusion.6.pick
  17.0 0.1 fusion.2
  17.1 0.6 broadcast_compare_fusion.1
  17.7 0.2 select_reduce_fusion.1
  17.9 0.7 select_reduce_fusion.4.own
  18.6 0.1 select_reduce_fusion.7
  18.7 0.8 select_reduce_fusion.high
  19.5 0.7 select_reduce_fusion.2.low
  20.2 0.6 select_select_fusion.link
  20.7 47.7 %collective-permute-done.refs_4_.refs_10_.refs_16_.refs_22_ = f32[8,5,128,128]{3,2,1,0:T(8,128)S(1)} collective-permute-done((f32[8,5,128,128]{3,2,1,0:T(8,128)}, f32[8,5,128,128]{3,2,1,0:T(8,128)S(1)}, u32[]{:S(2)}, u32[]{:S(2)}) %collective-permute-start) | collective-permute-done | bytes 2621472 | tf_op jit(solution)/shard_map/ppermute | solution.py:27
  68.5 0.0 copy-start
  68.5 1.8 %collective-permute-done.1.refs_5_.refs_11_.refs_17_.refs_23_ = f32[8,5,128,128]{3,2,1,0:T(8,128)} collective-permute-done((f32[8,5,128,128]{3,2,1,0:T(8,128)}, f32[8,5,128,128]{3,2,1,0:T(8,128)}, u32[]{:S(2)}, u32[]{:S(2)}) %collective-permute-start.1) | collective-permute-done | bytes 2621472 | tf_op jit(solution)/shard_map/ppermute | solution.py:27
  70.2 0.0 copy-done
  70.2 13.4 %settle.1 = (f32[32,128,128]{2,1,0:T(8,128)}, f32[32,2,128,128]{3,2,1,0:T(8,128)}, f32[32,128,128]{2,1,0:T(8,128)}, f32[32,128,128]{2,1,0:T(8,128)}, f32[14,32,1...) custom-call(s32[32]{0:T(128)} %get-tuple-element.118.mode, ...), custom_call_target="tpu_custom_call" | custom-call | tf_op jit(solution)/shard_map/settle/pallas_call | solution.py:179
  83.6 7.6 %exchange.4 = (f32[4,4,128]{2,1,0:T(4,128)}, f32[3,4,128]{2,1,0:T(4,128)}, f32[4,8,128]{2,1,0:T(8,128)}, f32[3,8,128]{2,1,0:T(8,128)}) custom-call(f32[3,4,128]{2,1,0:T(4,128)} %get-tuple-element.64.refs_0_, f32[4,4,128]{2,1,0:T(4,128)} %get-tuple-element.65.refs_1_, f32[3,8,128]{2,1,0:T(8,128)} %get-tuple-element.66.refs_2_, ...), custom_call_target="tpu_custom_call" | custom-call | tf_op jit(solution)/shard_map/exchange/pallas_call | solution.py:381
  91.2 0.7 broadcast_in_dim.137.refs_9_.refs_12_
  91.9 15.1 %step.4 = (f32[32,128,128]{2,1,0:T(8,128)}, f32[32,2,128,128]{3,2,1,0:T(8,128)}, f32[4,32,128]{2,1,0:T(8,128)}, f32[1,4,128]{2,1,0:T(4,128)}, f32[1,4,128]{2,1,0...) custom-call(s32[4,32]{1,0:T(4,128)} %select_select_fusion.link, ...), custom_call_target="tpu_custom_call" | custom-call | tf_op jit(solution)/shard_map/step/pallas_call | solution.py:321
  107.0 6.0 %exchange.5 = (f32[1,4,128]{2,1,0:T(4,128)}, f32[1,4,128]{2,1,0:T(4,128)}, f32[1,8,128]{2,1,0:T(8,128)}, f32[1,8,128]{2,1,0:T(8,128)}) custom-call(f32[1,4,128]{2,1,0:T(4,128)} %get-tuple-element.75.refs_0_, f32[1,4,128]{2,1,0:T(4,128)} %get-tuple-element.76.refs_1_, f32[1,8,128]{2,1,0:T(8,128)} %get-tuple-element.77.refs_2_, ...), custom_call_target="tpu_custom_call" | custom-call | tf_op jit(solution)/shard_map/exchange/pallas_call | solution.py:381
  113.0 12.8 %step.5 = (f32[32,128,128]{2,1,0:T(8,128)}, f32[32,2,128,128]{3,2,1,0:T(8,128)}, f32[4,32,128]{2,1,0:T(8,128)}, f32[1,4,128]{2,1,0:T(4,128)}, f32[1,4,128]{2,1,0...) custom-call(s32[4,32]{1,0:T(4,128)} %select_select_fusion.link, ...), custom_call_target="tpu_custom_call" | custom-call | tf_op jit(solution)/shard_map/step/pallas_call | solution.py:321
  125.8 5.4 %exchange.6 = (f32[1,4,128]{2,1,0:T(4,128)}, f32[1,4,128]{2,1,0:T(4,128)}, f32[1,8,128]{2,1,0:T(8,128)}, f32[1,8,128]{2,1,0:T(8,128)}) custom-call(f32[1,4,128]{2,1,0:T(4,128)} %get-tuple-element.89.refs_0_, f32[1,4,128]{2,1,0:T(4,128)} %get-tuple-element.90.refs_1_, f32[1,8,128]{2,1,0:T(8,128)} %get-tuple-element.91.refs_2_, ...), custom_call_target="tpu_custom_call" | custom-call | tf_op jit(solution)/shard_map/exchange/pallas_call | solution.py:381
  131.2 12.9 %step.6 = (f32[32,128,128]{2,1,0:T(8,128)}, f32[32,2,128,128]{3,2,1,0:T(8,128)}, f32[4,32,128]{2,1,0:T(8,128)}, f32[1,4,128]{2,1,0:T(4,128)}, f32[1,4,128]{2,1,0...) custom-call(s32[4,32]{1,0:T(4,128)} %select_select_fusion.link, ...), custom_call_target="tpu_custom_call" | custom-call | tf_op jit(solution)/shard_map/step/pallas_call | solution.py:321
  144.0 5.3 %exchange.7 = (f32[1,4,128]{2,1,0:T(4,128)}, f32[1,4,128]{2,1,0:T(4,128)}, f32[1,8,128]{2,1,0:T(8,128)}, f32[1,8,128]{2,1,0:T(8,128)}) custom-call(f32[1,4,128]{2,1,0:T(4,128)} %get-tuple-element.101.refs_0_, f32[1,4,128]{2,1,0:T(4,128)} %get-tuple-element.102.refs_1_, f32[1,8,128]{2,1,0:T(8,128)} %get-tuple-element.103.refs_2_, ...), custom_call_target="tpu_custom_call" | custom-call | tf_op jit(solution)/shard_map/exchange/pallas_call | solution.py:381
  149.4 11.7 %step.7 = (f32[32,128,128]{2,1,0:T(8,128)}, f32[32,2,128,128]{3,2,1,0:T(8,128)}, f32[4,32,128]{2,1,0:T(8,128)}) custom-call(s32[4,32]{1,0:T(4,128)} %select_select_fusion.link, s32[4,8]{1,0:T(4,128)} %select_reduce_fusion.6.pick, s32[32]{0:T(128)} %live.7, f32[32,128,128]{2,1,0:T(8,128)} %get-tuple-element.98.refs_0_, ...), custom_call_target="tpu_custom_call" | custom-call | tf_op jit(solution)/shard_map/step/pallas_call | solution.py:321
  (6 shorter events, 0.0 us)
Async XLA Ops:
  2.0 14.0 %copy-start.1 = (s32[32,4]{0,1:T(4,128)S(1)}, s32[32,4]{0,1:T(4,128)}, u32[]{:S(2)}) copy-start(s32[32,4]{0,1:T(4,128)} %param.12) | copy-start | bytes 1540
  9.5 59.0 %collective-permute-start = (f32[8,5,128,128]{3,2,1,0:T(8,128)}, f32[8,5,128,128]{3,2,1,0:T(8,128)S(1)}, u32[]{:S(2)}, u32[]{:S(2)}) collective-permute-start(f32[8,5,128,128]{3,2,1,0:T(8,128)} %get-tuple-element.57), channel_id=1, source_target_pairs={{0,1},{1,2},{2,3},{3,4},{4,5},{5,6},{6,7},{8,9},{9,10},{10,11},{11... | collective-permute-start | bytes 7864328 | tf_op jit(solution)/shard_map/ppermute | solution.py:27
  11.6 58.6 %collective-permute-start.1 = (f32[8,5,128,128]{3,2,1,0:T(8,128)}, f32[8,5,128,128]{3,2,1,0:T(8,128)}, u32[]{:S(2)}, u32[]{:S(2)}) collective-permute-start(f32[8,5,128,128]{3,2,1,0:T(8,128)} %get-tuple-element.58), channel_id=1, source_target_pairs={{1,0},{2,1},{3,2},{4,3},{5,4},{6,5},{7,6},{9,8},{10,9},{11,10},{12... | collective-permute-start | bytes 7864328 | tf_op jit(solution)/shard_map/ppermute | solution.py:27
  68.5 1.8 %copy-start = (f32[8,5,128,128]{3,2,1,0:T(8,128)}, f32[8,5,128,128]{3,2,1,0:T(8,128)S(1)}, u32[]{:S(2)}) copy-start(f32[8,5,128,128]{3,2,1,0:T(8,128)S(1)} %collective-permute-done.refs_4_.refs_10_.refs_16_.refs_22_) | copy-start | bytes 7864324

commit v5 on v4

--- a/solution.py
+++ b/solution.py
@@ -57,41 +57,52 @@
 LATER_KINDS = ((0,), (1,), (2,), (3,))
 
 
-def bundle_kernel(down, up, *refs):
-    ins, outs = refs[:8], refs[8:]
-    for way in range(2):
-        h, q, z, n = ins[4 * way : 4 * way + 4]
-        out = outs[way]
-        out[0, 0] = h[0]
-        out[0, 1] = q[0, 0]
-        out[0, 2] = q[0, 1]
-        out[0, 3] = z[0]
-        out[0, 4] = n[0]
+def bundle_kernel(group, down, up, *refs):
+    ins, outs = refs[: 8 * group], refs[8 * group :]
+    for i in range(group):
+        for way in range(2):
+            at = 8 * i + 4 * way
+            h, q, z, n = ins[at : at + 4]
+            out = outs[way]
+            out[i, 0] = h[0]
+            out[i, 1] = q[0, 0]
+            out[i, 2] = q[0, 1]
+            out[i, 3] = z[0]
+            out[i, 4] = n[0]
 
 
 def bundle(down, up, depth, discharge, bed, friction):
     tile = depth.shape[1]
     movers = down.shape[0]
-
-    def one(which):
-        return pl.BlockSpec((1, tile, tile), lambda m, d, u: ((d, u)[which][m], 0, 0))
-
-    def two(which):
-        return pl.BlockSpec((1, 2, tile, tile), lambda m, d, u: ((d, u)[which][m], 0, 0, 0))
-
-    out = pl.BlockSpec((1, 5, tile, tile), lambda m, d, u: (m, 0, 0, 0))
+    group = group_of(movers, 2)
+
+    def one(i, way):
+        return pl.BlockSpec(
+            (1, tile, tile), lambda m, *tables: (tables[way][m * group + i], 0, 0)
+        )
+
+    def two(i, way):
+        return pl.BlockSpec(
+            (1, 2, tile, tile), lambda m, *tables: (tables[way][m * group + i], 0, 0, 0)
+        )
+
+    ins = []
+    for i in range(group):
+        for way in range(2):
+            ins += [one(i, way), two(i, way), one(i, way), one(i, way)]
+    out = pl.BlockSpec((group, 5, tile, tile), lambda m, *_: (m, 0, 0, 0))
     shape = jax.ShapeDtypeStruct((movers, 5, tile, tile), F32)
     return pl.pallas_call(
-        bundle_kernel,
+        functools.partial(bundle_kernel, group),
         grid_spec=pltpu.PrefetchScalarGridSpec(
             num_scalar_prefetch=2,
-            grid=(movers,),
-            in_specs=[one(0), two(0), one(0), one(0), one(1), two(1), one(1), one(1)],
+            grid=(movers // group,),
+            in_specs=ins,
             out_specs=[out, out],
         ),
         out_shape=[shape, shape],
         name="bundle",
-    )(down, up, depth, discharge, bed, friction, depth, discharge, bed, friction)
+    )(down, up, *[depth, discharge, bed, friction] * (2 * group))
 
 
 def settle_kernel(group, mode, own, low, high, pick, *refs):

time: 162 us -> 161 us (level)
  Pallas kernels: 97.5 us -> 95.2 us
where the time goes in v5:
time: 161 us; the launch traced here: 159 us
  Pallas kernels  95.2 us (59%)
  waiting for transfers between devices  48.9 us (30%)
  starting transfers between devices  6.46 us (4%)
  other arithmetic  5.52 us (3%)
  local copies, waits for them, and re-layouts  2 us (1%)
    pallas_call x4, Pallas kernels, step(): pl.pallas_call(functools.partial(step_kernel, first, last), grid_spec=plt...  52.4 us
    ppermute x2, waiting for transfers between devices, neighbour(): return lax.ppermute(block, axis, route)  48.9 us
    pallas_call x4, Pallas kernels, exchange(): pl.pallas_call(functools.partial(exchange_kernel, extent), in_specs=[vmem...  23.1 us
    pallas_call x1, Pallas kernels, settle(): pl.pallas_call(functools.partial(settle_kernel, group), grid_spec=pltpu.P...  13.5 us
    ppermute x2, starting transfers between devices, neighbour(): return lax.ppermute(block, axis, route)  6.46 us
    pallas_call x1, Pallas kernels, bundle(): pl.pallas_call(functools.partial(bundle_kernel, group), grid_spec=pltpu.P...  6.16 us
  transfers between devices with their start and end apart: 2, of which 2 were waited for; matrix products, arithmetic and copies ran while one was open for 3% of the time, Pallas kernels for 0%

profile of v5, /device:TPU:4, one launch (start us, length us, event | category | flops | bytes accessed | tf_op | source)
XLA Modules:
  0.0 158.9 jit_solution(332292499564480729)
XLA Ops:
  0.6 0.8 compare_select_fusion.1
  1.4 0.6 slice_bitcast_fusion.2
  2.0 0.0 copy-start.1
  2.0 6.2 %bundle.1 = (f32[8,5,128,128]{3,2,1,0:T(8,128)}, f32[8,5,128,128]{3,2,1,0:T(8,128)}) custom-call(s32[8]{0:T(128)} %get-tuple-element.122.down, s32[8]{0:T(128)} %get-tuple-element.121.up, f32[32,128,128]{2,1,0:T(8,128)} %refs_18_.1, f32[32,2,128,128]{3,2,1,0:T(8,128)} %refs_19_.1, f32[32,128,128]{2,1,0:T(8,128)} %refs_20_.1, f32[32,128,128]{2,1,0:T(8,128)} %refs_21_.1, ...), custom_call_target="tpu_custom_call" | custom-call | tf_op jit(solution)/shard_map/bundle/pallas_call | solution.py:95
  8.2 1.9 %collective-permute-start = (f32[8,5,128,128]{3,2,1,0:T(8,128)}, f32[8,5,128,128]{3,2,1,0:T(8,128)S(1)}, u32[]{:S(2)}, u32[]{:S(2)}) collective-permute-start(f32[8,5,128,128]{3,2,1,0:T(8,128)} %get-tuple-element.57), channel_id=1, source_target_pairs={{0,1},{1,2},{2,3},{3,4},{4,5},{5,6},{6,7},{8,9},{9,10},{10,11},{11... | collective-permute-start | bytes 7864328 | tf_op jit(solution)/shard_map/ppermute | solution.py:27
  10.1 4.5 %collective-permute-start.1 = (f32[8,5,128,128]{3,2,1,0:T(8,128)}, f32[8,5,128,128]{3,2,1,0:T(8,128)}, u32[]{:S(2)}, u32[]{:S(2)}) collective-permute-start(f32[8,5,128,128]{3,2,1,0:T(8,128)} %get-tuple-element.58), channel_id=1, source_target_pairs={{1,0},{2,1},{3,2},{4,3},{5,4},{6,5},{7,6},{9,8},{10,9},{11,10},{12... | collective-permute-start | bytes 7864328 | tf_op jit(solution)/shard_map/ppermute | solution.py:27
  14.7 0.0 copy-done.1
  14.7 0.3 convert_reduce_fusion
  15.0 0.7 select_reduce_fusion.6.pick
  15.7 0.1 fusion.2
  15.8 0.6 broadcast_compare_fusion.1
  16.4 0.2 select_reduce_fusion.1
  16.6 0.7 select_reduce_fusion.4.own
  17.3 0.1 select_reduce_fusion.7
  17.4 0.8 select_reduce_fusion.high
  18.2 0.7 select_reduce_fusion.2.low
  18.9 0.6 select_select_fusion.link
  19.5 48.1 %collective-permute-done.refs_4_.refs_10_.refs_16_.refs_22_ = f32[8,5,128,128]{3,2,1,0:T(8,128)S(1)} collective-permute-done((f32[8,5,128,128]{3,2,1,0:T(8,128)}, f32[8,5,128,128]{3,2,1,0:T(8,128)S(1)}, u32[]{:S(2)}, u32[]{:S(2)}) %collective-permute-start) | collective-permute-done | bytes 2621472 | tf_op jit(solution)/shard_map/ppermute | solution.py:27
  67.5 0.0 copy-start
  67.5 0.9 collective-permute-done.1.refs_5_.refs_11_.refs_17_.refs_23_
  68.4 0.7 copy-done
  69.1 13.5 %settle.1 = (f32[32,128,128]{2,1,0:T(8,128)}, f32[32,2,128,128]{3,2,1,0:T(8,128)}, f32[32,128,128]{2,1,0:T(8,128)}, f32[32,128,128]{2,1,0:T(8,128)}, f32[14,32,1...) custom-call(s32[32]{0:T(128)} %get-tuple-element.118.mode, ...), custom_call_target="tpu_custom_call" | custom-call | tf_op jit(solution)/shard_map/settle/pallas_call | solution.py:190
  82.6 6.8 %exchange.4 = (f32[4,4,128]{2,1,0:T(4,128)}, f32[3,4,128]{2,1,0:T(4,128)}, f32[4,8,128]{2,1,0:T(8,128)}, f32[3,8,128]{2,1,0:T(8,128)}) custom-call(f32[3,4,128]{2,1,0:T(4,128)} %get-tuple-element.64.refs_0_, f32[4,4,128]{2,1,0:T(4,128)} %get-tuple-element.65.refs_1_, f32[3,8,128]{2,1,0:T(8,128)} %get-tuple-element.66.refs_2_, ...), custom_call_target="tpu_custom_call" | custom-call | tf_op jit(solution)/shard_map/exchange/pallas_call | solution.py:392
  89.4 0.7 broadcast_in_dim.137.refs_9_.refs_12_
  90.1 15.1 %step.4 = (f32[32,128,128]{2,1,0:T(8,128)}, f32[32,2,128,128]{3,2,1,0:T(8,128)}, f32[4,32,128]{2,1,0:T(8,128)}, f32[1,4,128]{2,1,0:T(4,128)}, f32[1,4,128]{2,1,0...) custom-call(s32[4,32]{1,0:T(4,128)} %select_select_fusion.link, ...), custom_call_target="tpu_custom_call" | custom-call | tf_op jit(solution)/shard_map/step/pallas_call | solution.py:332
  105.2 5.6 %exchange.5 = (f32[1,4,128]{2,1,0:T(4,128)}, f32[1,4,128]{2,1,0:T(4,128)}, f32[1,8,128]{2,1,0:T(8,128)}, f32[1,8,128]{2,1,0:T(8,128)}) custom-call(f32[1,4,128]{2,1,0:T(4,128)} %get-tuple-element.75.refs_0_, f32[1,4,128]{2,1,0:T(4,128)} %get-tuple-element.76.refs_1_, f32[1,8,128]{2,1,0:T(8,128)} %get-tuple-element.77.refs_2_, ...), custom_call_target="tpu_custom_call" | custom-call | tf_op jit(solution)/shard_map/exchange/pallas_call | solution.py:392
  110.9 12.8 %step.5 = (f32[32,128,128]{2,1,0:T(8,128)}, f32[32,2,128,128]{3,2,1,0:T(8,128)}, f32[4,32,128]{2,1,0:T(8,128)}, f32[1,4,128]{2,1,0:T(4,128)}, f32[1,4,128]{2,1,0...) custom-call(s32[4,32]{1,0:T(4,128)} %select_select_fusion.link, ...), custom_call_target="tpu_custom_call" | custom-call | tf_op jit(solution)/shard_map/step/pallas_call | solution.py:332
  123.7 5.4 %exchange.6 = (f32[1,4,128]{2,1,0:T(4,128)}, f32[1,4,128]{2,1,0:T(4,128)}, f32[1,8,128]{2,1,0:T(8,128)}, f32[1,8,128]{2,1,0:T(8,128)}) custom-call(f32[1,4,128]{2,1,0:T(4,128)} %get-tuple-element.89.refs_0_, f32[1,4,128]{2,1,0:T(4,128)} %get-tuple-element.90.refs_1_, f32[1,8,128]{2,1,0:T(8,128)} %get-tuple-element.91.refs_2_, ...), custom_call_target="tpu_custom_call" | custom-call | tf_op jit(solution)/shard_map/exchange/pallas_call | solution.py:392
  129.0 12.9 %step.6 = (f32[32,128,128]{2,1,0:T(8,128)}, f32[32,2,128,128]{3,2,1,0:T(8,128)}, f32[4,32,128]{2,1,0:T(8,128)}, f32[1,4,128]{2,1,0:T(4,128)}, f32[1,4,128]{2,1,0...) custom-call(s32[4,32]{1,0:T(4,128)} %select_select_fusion.link, ...), custom_call_target="tpu_custom_call" | custom-call | tf_op jit(solution)/shard_map/step/pallas_call | solution.py:332
  141.9 5.3 %exchange.7 = (f32[1,4,128]{2,1,0:T(4,128)}, f32[1,4,128]{2,1,0:T(4,128)}, f32[1,8,128]{2,1,0:T(8,128)}, f32[1,8,128]{2,1,0:T(8,128)}) custom-call(f32[1,4,128]{2,1,0:T(4,128)} %get-tuple-element.101.refs_0_, f32[1,4,128]{2,1,0:T(4,128)} %get-tuple-element.102.refs_1_, f32[1,8,128]{2,1,0:T(8,128)} %get-tuple-element.103.refs_2_, ...), custom_call_target="tpu_custom_call" | custom-call | tf_op jit(solution)/shard_map/exchange/pallas_call | solution.py:392
  147.2 11.7 %step.7 = (f32[32,128,128]{2,1,0:T(8,128)}, f32[32,2,128,128]{3,2,1,0:T(8,128)}, f32[4,32,128]{2,1,0:T(8,128)}) custom-call(s32[4,32]{1,0:T(4,128)} %select_select_fusion.link, s32[4,8]{1,0:T(4,128)} %select_reduce_fusion.6.pick, s32[32]{0:T(128)} %live.7, f32[32,128,128]{2,1,0:T(8,128)} %get-tuple-element.98.refs_0_, ...), custom_call_target="tpu_custom_call" | custom-call | tf_op jit(solution)/shard_map/step/pallas_call | solution.py:332
  (6 shorter events, 0.0 us)
Async XLA Ops:
  2.0 12.7 %copy-start.1 = (s32[32,4]{0,1:T(4,128)S(1)}, s32[32,4]{0,1:T(4,128)}, u32[]{:S(2)}) copy-start(s32[32,4]{0,1:T(4,128)} %param.12) | copy-start | bytes 1540
  8.2 59.4 %collective-permute-start = (f32[8,5,128,128]{3,2,1,0:T(8,128)}, f32[8,5,128,128]{3,2,1,0:T(8,128)S(1)}, u32[]{:S(2)}, u32[]{:S(2)}) collective-permute-start(f32[8,5,128,128]{3,2,1,0:T(8,128)} %get-tuple-element.57), channel_id=1, source_target_pairs={{0,1},{1,2},{2,3},{3,4},{4,5},{5,6},{6,7},{8,9},{9,10},{10,11},{11... | collective-permute-start | bytes 7864328 | tf_op jit(solution)/shard_map/ppermute | solution.py:27
  10.1 58.3 %collective-permute-start.1 = (f32[8,5,128,128]{3,2,1,0:T(8,128)}, f32[8,5,128,128]{3,2,1,0:T(8,128)}, u32[]{:S(2)}, u32[]{:S(2)}) collective-permute-start(f32[8,5,128,128]{3,2,1,0:T(8,128)} %get-tuple-element.58), channel_id=1, source_target_pairs={{1,0},{2,1},{3,2},{4,3},{5,4},{6,5},{7,6},{9,8},{10,9},{11,10},{12... | collective-permute-start | bytes 7864328 | tf_op jit(solution)/shard_map/ppermute | solution.py:27
  67.5 1.5 copy-start
